TPU v7x, 128 devices: a whole 4x4x4 slice. The times are simulated.
128 devices in a mesh: sec: 64 (over y, z, x), mpo: 2 (over core).
Axes of the slice: x: 4, y: 4, z: 4, core: 2. Of those that a mesh axis runs over, the one named last changes fastest.
Arguments:
- sector_dims: int32 [3072], P('sec'), may hold values from 1 to 256, 688128 in all
- new_owner: int32 [3072], P('sec'), may hold values from 0 to 63, as said below
- new_slot: int32 [3072], P('sec'), may hold values from 0 to 47, as said below
- block_pairs: int32 [3072, 4], P('sec', 'mpo'), may hold values from 0 to 47
- theta_blocks: bfloat16 [3072, 256, 256], P('sec'), may hold values from -6 to 6
- left_env: bfloat16 [3072, 4, 256, 256], P('sec', 'mpo'), may hold values from -0.1875 to 0.1875
- right_env: bfloat16 [4, 256, 256], P('mpo'), may hold values from -0.375 to 0.375
Outputs:
- applied: bfloat16 [256, 3072, 256], P('mpo', 'sec')
Inputs may be any that keep to these rules, and one draw needn't show every extreme that they name: Rows 0 to sector_dims - 1 of a block are live; the largest equals 256. `new_owner`: every index of sec receives exactly 48 blocks; one index sends at most 1 block to any one index, and exactly 1 to some. `new_slot`: the blocks that one index receives take its 48 slots once each. `block_pairs`: partners are slots of the same index of sec as the block.
All inputs are finite; a program needn't handle non-finite values.
Results may differ from a plain program's by a relative error of at most 0.0049.
Values may be sent and summed in bfloat16 or wider, within the bound.
No kernel may reach another device: no remote copies, remote signals or barrier semaphores. Data moves between devices by JAX's collectives and lax.ppermute only.
A program may use at most 192 MiB of HBM per device.

v0:
```python
import jax
import jax.numpy as jnp
from jax import lax
from jax.sharding import PartitionSpec as P


def live_rows(blocks, sector_dims, extra):
    row_ids = jnp.arange(blocks.shape[-2], dtype=jnp.int32)
    keep = row_ids[None, :] < sector_dims[:, None]
    shaped = keep.reshape((keep.shape[0],) + (1,) * extra + (keep.shape[1], 1))
    return jnp.where(shaped, blocks, jnp.zeros((), blocks.dtype))


def on_device(sector_dims, new_owner, new_slot, block_pairs, theta_blocks, left_env, right_env):
    peers = lax.axis_size("sec")
    slots = theta_blocks.shape[0]
    per_peer = (slots + peers - 1) // peers
    theta_live = live_rows(theta_blocks, sector_dims, 0)
    left_live = live_rows(left_env, sector_dims, 1)
    chosen = (new_owner[None, :] == jnp.arange(peers, dtype=jnp.int32)[:, None]).astype(jnp.int32)
    ranked = jnp.cumsum(chosen, axis=1) - 1
    select = chosen[:, None, :] * (
        ranked[:, None, :] == jnp.arange(per_peer, dtype=jnp.int32)[None, :, None]
    ).astype(jnp.int32)
    present = (jnp.sum(select, axis=2) > 0).reshape(peers * per_peer)
    source_slot = jnp.sum(
        select * jnp.arange(slots, dtype=jnp.int32)[None, None, :], axis=2
    ).reshape(peers * per_peer)
    target_slot = jnp.where(
        present, jnp.sum(select * new_slot[None, None, :], axis=2).reshape(peers * per_peer), -1
    )

    def outgoing(blocks):
        picked = jnp.take(blocks, source_slot, axis=0)
        shaped = present.reshape((peers * per_peer,) + (1,) * (blocks.ndim - 1))
        return jnp.where(shaped, picked, jnp.zeros((), blocks.dtype))

    def arrange(received, arrived_slot):
        match = (arrived_slot[None, :] == jnp.arange(slots, dtype=jnp.int32)[:, None]).astype(
            jnp.int32
        )
        anchor = jnp.sum(
            match * jnp.arange(arrived_slot.shape[0], dtype=jnp.int32)[None, :], axis=1
        )
        return jnp.take(received, anchor, axis=0)

    got_theta, got_left, arrived = (
        lax.all_to_all(outgoing(theta_live), "sec", split_axis=0, concat_axis=0, tiled=True),
        lax.all_to_all(outgoing(left_live), "sec", split_axis=0, concat_axis=0, tiled=True),
        lax.all_to_all(target_slot, "sec", split_axis=0, concat_axis=0, tiled=True),
    )
    transfer = jnp.einsum(
        "prc,wcn->pwrn", arrange(got_theta, arrived), right_env, preferred_element_type=jnp.float32
    ).astype(jnp.bfloat16)
    left_new = arrange(got_left, arrived)
    channel = jnp.arange(block_pairs.shape[1], dtype=jnp.int32)[None, :]
    partner = transfer[block_pairs, channel]
    applied = lax.psum_scatter(
        jnp.einsum("swrc,swcn->rsn", left_new, partner, preferred_element_type=jnp.float32),
        "mpo",
        scatter_dimension=0,
        tiled=True,
    )
    return applied.astype(jnp.bfloat16)


def solution(mesh):
    return jax.shard_map(
        on_device,
        mesh=mesh,
        in_specs=(
            P("sec"),
            P("sec"),
            P("sec"),
            P("sec", "mpo"),
            P("sec", None, None),
            P("sec", "mpo", None, None),
            P("mpo", None, None),
        ),
        out_specs=P("mpo", "sec", None),
        check_vma=False,
    )
```

profile of v0, /device:TPU:11, one launch (start us, length us, event | category | flops | bytes accessed | tf_op | source)
XLA Modules:
  0.0 492.4 jit_solution(12682370928830417412)
XLA Ops:
  6.5 0.7 fusion.12
  7.2 0.2 reduce_window_sum.11
  7.5 0.8 multiply_reduce_fusion.1
  8.2 0.8 select_reduce_fusion
  9.0 0.7 copy.22
  9.8 10.8 %all-to-all-start = ((s32[64,1,1]{2,1,0:T(1,128)}), s32[64,1,1]{2,1,0:T(1,128)S(1)}, u32[]{:S(2)}, u32[]{:S(2)}) async-start(s32[64,1,1]{2,1,0:T(1,128)} %copy.22), calls=%async_computation | async-start | bytes 65536 | tf_op jit(solution)/shard_map/all_to_all | solution.py:50
  20.6 0.7 iota_compare_fusion
  21.4 7.6 %broadcast_select_fusion.1 = bf16[48,256,256]{2,1,0:T(8,128)(2,1)} fusion(bf16[48,256,256]{2,1,0:T(8,128)(2,1)} %param.11, pred[48,256]{1,0:T(8,128)(4,1)S(1)} %iota_compare_fusion), kind=kLoop, calls=%fused_computation.16 | loop fusion | flops 3145728 | bytes 12595200 | tf_op jit(solution)/shard_map/jit(_where)/select_n | solution.py:11
  29.0 8.3 %gather_fusion = bf16[64,256,256]{2,1,0:T(8,128)(2,1)} fusion(bf16[48,256,256]{2,1,0:T(8,128)(2,1)} %broadcast_select_fusion.1, s32[1024]{0:T(1024)S(1)} %pad_clamp_fusion.1), kind=kCustom, calls=%fused_computation | custom fusion | bytes 16777472 | tf_op jit(solution)/shard_map/jit(_take)/gather | solution.py:34
  37.3 7.6 %select_select_fusion.1 = bf16[64,256,256]{2,1,0:T(8,128)(2,1)} fusion(bf16[64,256,256]{2,1,0:T(8,128)(2,1)} %gather_fusion, pred[64]{0:T(512)(128)(4,1)S(1)} %get-tuple-element.9, pred[64]{0:T(512)(128)(4,1)S(1)} %get-tuple-element.10), kind=kLoop, calls=%fused_computation.11 | loop fusion | flops 8388608 | bytes 16777344 | tf_op jit(solution)/shard_map/jit(_where)/select_n | solution.py:36
  44.8 0.0 all-to-all-done
  44.8 10.0 %all-to-all-start.1 = ((bf16[64,256,256]{2,1,0:T(8,128)(2,1)}), bf16[64,256,256]{2,1,0:T(8,128)(2,1)}, u32[]{:S(2)}, u32[]{:S(2)}) async-start(bf16[64,256,256]{2,1,0:T(8,128)(2,1)} %select_select_fusion.1), calls=%async_computation.1 | async-start | bytes 16777216 | tf_op jit(solution)/shard_map/all_to_all | solution.py:48
  54.8 10.9 %broadcast_select_fusion = bf16[48,2,256,256]{3,2,1,0:T(8,128)(2,1)} fusion(bf16[48,2,256,256]{3,2,1,0:T(8,128)(2,1)} %param.12, pred[48,256]{1,0:T(8,128)(4,1)S(1)} %iota_compare_fusion), kind=kLoop, calls=%fused_computation.10 | loop fusion | flops 6291456 | bytes 25178112 | tf_op jit(solution)/shard_map/jit(_where)/select_n | solution.py:11
  65.8 12.1 %gather_fusion.3 = bf16[64,2,256,256]{3,2,1,0:T(8,128)(2,1)} fusion(bf16[48,2,256,256]{3,2,1,0:T(8,128)(2,1)} %broadcast_select_fusion, s32[1024]{0:T(1024)S(1)} %pad_clamp_fusion.1), kind=kCustom, calls=%fused_computation.3 | custom fusion | bytes 33554688 | tf_op jit(solution)/shard_map/jit(_take)/gather | solution.py:34
  77.9 14.3 %select_select_fusion = bf16[64,2,256,256]{3,2,1,0:T(8,128)(2,1)} fusion(bf16[64,2,256,256]{3,2,1,0:T(8,128)(2,1)} %gather_fusion.3, pred[64]{0:T(512)(128)(4,1)S(1)} %get-tuple-element.9, pred[64]{0:T(512)(128)(4,1)S(1)} %get-tuple-element.10), kind=kLoop, calls=%fused_computation.5 | loop fusion | flops 16777216 | bytes 33554560 | tf_op jit(solution)/shard_map/jit(_where)/select_n | solution.py:36
  92.2 67.1 %all-to-all-done.1 = bf16[64,256,256]{2,1,0:T(8,128)(2,1)} async-done(((bf16[64,256,256]{2,1,0:T(8,128)(2,1)}), bf16[64,256,256]{2,1,0:T(8,128)(2,1)}, u32[]{:S(2)}, u32[]{:S(2)}) %all-to-all-start.1) | async-done | bytes 8388640 | tf_op jit(solution)/shard_map/all_to_all | solution.py:48
  159.3 11.8 %all-to-all-start.2 = ((bf16[64,2,256,256]{3,2,1,0:T(8,128)(2,1)}), bf16[64,2,256,256]{3,2,1,0:T(8,128)(2,1)}, u32[]{:S(2)}, u32[]{:S(2)}) async-start(bf16[64,2,256,256]{3,2,1,0:T(8,128)(2,1)} %select_select_fusion), calls=%async_computation.2 | async-start | bytes 33554432 | tf_op jit(solution)/shard_map/all_to_all | solution.py:49
  171.1 0.2 reduce-scatter.2.cloned.1.call-start
  171.3 0.1 copy.23
  171.4 0.1 reshape.241
  171.5 1.2 reduce.4
  172.8 0.1 select_reduce_fusion.1
  172.9 8.4 %gather_fusion.1 = bf16[48,256,256]{2,1,0:T(8,128)(2,1)} fusion(bf16[64,256,256]{2,1,0:T(8,128)(2,1)} %all-to-all-done.1, s32[1024]{0:T(1024)S(1)} %pad_clamp_fusion), kind=kCustom, calls=%fused_computation.1 | custom fusion | bytes 12583104 | tf_op jit(solution)/shard_map/jit(_take)/gather | solution.py:45
  181.4 9.2 %convert_bitcast_fusion = bf16[48,2,256,256]{3,2,1,0:T(8,128)(2,1)} fusion(bf16[48,256,256]{2,1,0:T(8,128)(2,1)} %gather_fusion.1, pred[48]{0:T(512)(128)(4,1)S(1)} %compare_and_fusion.1, bf16[2,256,256]{2,1,0:T(8,128)(2,1)S(1)} %copy-done), kind=kOutput, calls=%fused_computation.8 | convolution fusion | flops 3230662656 | bytes 19136560 | tf_op jit(solution)/shard_map/prc,wcn->pwrn/dot_general | solution.py:52
  190.6 11.6 %gather_fusion.2 = bf16[96,256,256]{2,1,0:T(8,128)(2,1)} fusion(bf16[48,2,256,256]{3,2,1,0:T(8,128)(2,1)} %convert_bitcast_fusion, s32[96]{0:T(128)S(1)} %reshape.241), kind=kCustom, calls=%fused_computation.2 | custom fusion | bytes 25166592 | tf_op jit(solution)/shard_map/gather | solution.py:57
  202.2 198.8 %all-to-all-done.2 = bf16[64,2,256,256]{3,2,1,0:T(8,128)(2,1)} async-done(((bf16[64,2,256,256]{3,2,1,0:T(8,128)(2,1)}), bf16[64,2,256,256]{3,2,1,0:T(8,128)(2,1)}, u32[]{:S(2)}, u32[]{:S(2)}) %all-to-all-start.2) | async-done | bytes 16777248 | tf_op jit(solution)/shard_map/all_to_all | solution.py:49
  401.0 12.1 %gather_fusion.4 = bf16[48,2,256,256]{3,2,1,0:T(8,128)(2,1)} fusion(bf16[64,2,256,256]{3,2,1,0:T(8,128)(2,1)} %all-to-all-done.2, s32[1024]{0:T(1024)S(1)} %pad_clamp_fusion), kind=kCustom, calls=%fused_computation.4 | custom fusion | bytes 25166016 | tf_op jit(solution)/shard_map/jit(_take)/gather | solution.py:45
  413.1 15.1 %fusion.7 = f32[256,48,256]{0,2,1:T(8,128)} fusion(bf16[48,2,256,256]{3,2,1,0:T(8,128)(2,1)} %bitcast.35, bf16[48,2,256,256]{3,2,1,0:T(8,128)(2,1)} %gather_fusion.4, pred[48]{0:T(512)(128)(4,1)S(1)} %compare_and_fusion.1), kind=kOutput, calls=%fused_computation.17 | convolution fusion | flops 3227516928 | bytes 37748784 | tf_op jit(solution)/shard_map/swrc,swcn->rsn/dot_general | solution.py:59
  428.2 0.0 reduce-scatter.2.cloned.1.call-update
  428.2 51.0 %reduce-scatter.2.cloned.1.call-done = f32[128,48,256]{0,2,1:T(8,128)} async-done(((f32[256,48,256]{0,2,1:T(8,128)}), f32[128,48,256]{0,2,1:T(8,128)}) %reduce-scatter.2.cloned.1.call-update) | async-done | bytes 6291472 | tf_op jit(solution)/shard_map/reduce_scatter | solution.py:58
  479.2 3.3 convert_element_type.33
  482.5 3.0 copy.25
  (12 shorter events, 0.1 us)
Async XLA Ops:
  6.5 174.8 %copy-start = (bf16[2,256,256]{2,1,0:T(8,128)(2,1)S(1)}, bf16[2,256,256]{2,1,0:T(8,128)(2,1)}, u32[]{:S(2)}) copy-start(bf16[2,256,256]{2,1,0:T(8,128)(2,1)} %param.13) | copy-start | bytes 786436
  9.8 35.1 %all-to-all-start = ((s32[64,1,1]{2,1,0:T(1,128)}), s32[64,1,1]{2,1,0:T(1,128)S(1)}, u32[]{:S(2)}, u32[]{:S(2)}) async-start(s32[64,1,1]{2,1,0:T(1,128)} %copy.22), calls=%async_computation | async-start | bytes 65536 | tf_op jit(solution)/shard_map/all_to_all | solution.py:50
  44.8 114.4 %all-to-all-start.1 = ((bf16[64,256,256]{2,1,0:T(8,128)(2,1)}), bf16[64,256,256]{2,1,0:T(8,128)(2,1)}, u32[]{:S(2)}, u32[]{:S(2)}) async-start(bf16[64,256,256]{2,1,0:T(8,128)(2,1)} %select_select_fusion.1), calls=%async_computation.1 | async-start | bytes 16777216 | tf_op jit(solution)/shard_map/all_to_all | solution.py:48
  92.2 79.1 %copy-start.1 = (s32[48,2]{0,1:T(2,128)S(1)}, s32[48,2]{0,1:T(2,128)}, u32[]{:S(2)}) copy-start(s32[48,2]{0,1:T(2,128)} %param.10) | copy-start | bytes 1156
  159.3 241.7 %all-to-all-start.2 = ((bf16[64,2,256,256]{3,2,1,0:T(8,128)(2,1)}), bf16[64,2,256,256]{3,2,1,0:T(8,128)(2,1)}, u32[]{:S(2)}, u32[]{:S(2)}) async-start(bf16[64,2,256,256]{3,2,1,0:T(8,128)(2,1)} %select_select_fusion), calls=%async_computation.2 | async-start | bytes 33554432 | tf_op jit(solution)/shard_map/all_to_all | solution.py:49
  171.1 308.2 %reduce-scatter.2.cloned.1.call-start = ((), (), s32[]{:S(2)}) async-start(), calls=%async_computation.4 | async-start | bytes 18874368 | tf_op jit(solution)/shard_map/reduce_scatter | solution.py:58
Sparse Core Ops, SparseCore 0:
  428.3 50.8 reduce-scatter.1
where the time goes:
time: 494 us; the launch traced here: 492 us
  waiting for transfers between devices  317 us (64%)
  local copies, waits for them, and re-layouts  56.5 us (11%)
  other arithmetic  48.4 us (10%)
  starting transfers between devices  32.8 us (7%)
  matrix products  24.3 us (5%)
  between operations  13.5 us (3%)
    all_to_all x1, waiting for transfers between devices, on_device(): lax.all_to_all(outgoing(left_live), 'sec', split_axis=0, concat_axis=0, t...  199 us
    all_to_all x1, waiting for transfers between devices, on_device(): lax.all_to_all(outgoing(theta_live), 'sec', split_axis=0, concat_axis=0,...  67.1 us
    reduce_scatter x1, waiting for transfers between devices, on_device(): lax.psum_scatter(jnp.einsum('swrc,swcn->rsn', left_new, partner, preferre...  51 us
    select_n x2, other arithmetic, outgoing(): return jnp.where(shaped, picked, jnp.zeros((), blocks.dtype))  21.9 us
    gather x2, local copies, waits for them, and re-layouts, arrange(): return jnp.take(received, anchor, axis=0)  20.6 us
    gather x2, local copies, waits for them, and re-layouts, outgoing(): picked = jnp.take(blocks, source_slot, axis=0)  20.4 us
    select_n x2, other arithmetic, live_rows(): return jnp.where(shaped, blocks, jnp.zeros((), blocks.dtype))  18.6 us
    dot_general x1, matrix products, on_device(): jnp.einsum('swrc,swcn->rsn', left_new, partner, preferred_element_type=jn...  15.1 us
  transfers between devices with their start and end apart: 4, of which 3 were waited for; matrix products, arithmetic and copies ran while one was open for 19% of the time, Pallas kernels for 0%

commit v1 on v0

v1 whole, which is shorter than its diff:
```python
import functools

import jax
import jax.numpy as jnp
from jax import lax
from jax.experimental import pallas as pl
from jax.experimental.pallas import tpu as pltpu
from jax.sharding import PartitionSpec as P

SWAP = [(0, 1), (1, 0)]
GROUP = 16


def pack_kernel(owner_ref, core_ref, theta_ref, left_ref, out_ref, sems):
    slots, channels, tile, _ = left_ref.shape
    half, quarter = tile // 2, tile // 4
    core = core_ref[0]

    def send(i, carry):
        owner = owner_ref[i]
        for h in range(2):
            place = 2 * owner + h
            for w in range(channels):
                pltpu.make_async_copy(
                    left_ref.at[i, w, pl.ds(h * half, half)],
                    out_ref.at[place, pl.ds(w * half, half)],
                    sems.at[i],
                ).start()
            first = pl.multiple_of(h * half + core * quarter, quarter)
            pltpu.make_async_copy(
                theta_ref.at[i, pl.ds(first, quarter)],
                out_ref.at[place, pl.ds(channels * half, quarter)],
                sems.at[i],
            ).start()
        return carry

    lax.fori_loop(0, slots, send, 0)

    def settle(i, carry):
        pair = out_ref.at[pl.ds(2 * owner_ref[i], 2)]
        pltpu.make_async_copy(pair, pair, sems.at[i]).wait()
        return carry

    lax.fori_loop(0, slots, settle, 0)


def pack(new_owner, core, theta_blocks, left_env, peers):
    slots, channels, tile, cols = left_env.shape
    rows = channels * tile // 2 + tile // 4
    moved = 2 * slots * 2 * rows * cols * 2
    return pl.pallas_call(
        pack_kernel,
        grid_spec=pltpu.PrefetchScalarGridSpec(
            num_scalar_prefetch=2,
            grid=(),
            in_specs=[pl.BlockSpec(memory_space=pltpu.HBM)] * 2,
            out_specs=pl.BlockSpec(memory_space=pltpu.HBM),
            scratch_shapes=[pltpu.SemaphoreType.DMA((slots,))],
        ),
        out_shape=jax.ShapeDtypeStruct((2 * peers, rows, cols), theta_blocks.dtype),
        cost_estimate=pl.CostEstimate(flops=0, bytes_accessed=moved, transcendentals=0),
        name="pack_parcels",
    )(new_owner, core, theta_blocks, left_env)


def apply_kernel(
    anchor_ref, dims_ref, pairs_ref, core_ref,
    got_ref, other_ref, right_ref, out_ref,
    theta, left, transfer, rows_f32, theta_sems, left_sems,
):
    slots, tile, cols = theta.shape
    channels = right_ref.shape[0]
    half, quarter = tile // 2, tile // 4
    core = core_ref[0]
    bulk = got_ref.shape[1] - quarter

    def fetch_theta(j, carry):
        source = anchor_ref[j]
        for c in range(2):
            mine = pl.multiple_of(core * half + c * quarter, quarter)
            theirs = pl.multiple_of((1 - core) * half + c * quarter, quarter)
            pltpu.make_async_copy(
                got_ref.at[2 * source + c, pl.ds(bulk, quarter)],
                theta.at[j, pl.ds(mine, quarter)],
                theta_sems.at[j],
            ).start()
            pltpu.make_async_copy(
                other_ref.at[2 * source + c],
                theta.at[j, pl.ds(theirs, quarter)],
                theta_sems.at[j],
            ).start()
        return carry

    def fetch_left(j, carry):
        source = anchor_ref[j]
        for c in range(2):
            pltpu.make_async_copy(
                got_ref.at[2 * source + c, pl.ds(0, bulk)],
                left.at[j, pl.ds(c * bulk, bulk)],
                left_sems.at[j],
            ).start()
        return carry

    lax.fori_loop(0, slots, fetch_theta, 0)
    lax.fori_loop(0, slots, fetch_left, 0)

    row_ids = lax.broadcasted_iota(jnp.int32, (tile, cols), 0)

    def build(j, carry):
        pltpu.make_async_copy(theta.at[j], theta.at[j], theta_sems.at[j]).wait()
        live = jnp.where(row_ids < dims_ref[j], theta[j].astype(jnp.float32), 0.0)
        live = live.astype(theta.dtype)
        for w in range(channels):
            transfer[j, w] = jnp.dot(
                live, right_ref[w], preferred_element_type=jnp.float32
            ).astype(transfer.dtype)
        return carry

    lax.fori_loop(0, slots, build, 0)

    half_ids = lax.broadcasted_iota(jnp.int32, (half, cols), 0) + core * half

    for g in range(slots // GROUP):

        def contract(k, carry):
            j = g * GROUP + k
            pltpu.make_async_copy(left.at[j], left.at[j], left_sems.at[j]).wait()
            total = jnp.zeros((half, cols), jnp.float32)
            for w in range(channels):
                total += jnp.dot(
                    left[j, w * half:(w + 1) * half],
                    transfer[pairs_ref[w, j], w],
                    preferred_element_type=jnp.float32,
                )
            total = jnp.where(half_ids < dims_ref[j], total, 0.0)
            rows_f32[:, pl.ds(k, half, stride=GROUP)] = jnp.stack(
                [total[:, :128], total[:, 128:]]
            )
            return carry

        lax.fori_loop(0, GROUP, contract, 0)
        for side in range(2):
            out_ref[:, g * GROUP:(g + 1) * GROUP, side * 128:(side + 1) * 128] = (
                rows_f32[side].reshape(half, GROUP, 128).astype(out_ref.dtype)
            )


def apply(anchor, dims, pairs, core, got, other, right, dtype):
    channels, tile, cols = right.shape
    slots = anchor.shape[0]
    half = tile // 2
    flops = 2 * slots * channels * (tile + half) * tile * cols
    moved = 2 * slots * cols * (tile + channels * half + half)
    return pl.pallas_call(
        apply_kernel,
        grid_spec=pltpu.PrefetchScalarGridSpec(
            num_scalar_prefetch=4,
            grid=(),
            in_specs=[
                pl.BlockSpec(memory_space=pltpu.HBM),
                pl.BlockSpec(memory_space=pltpu.HBM),
                pl.BlockSpec(memory_space=pltpu.VMEM),
            ],
            out_specs=pl.BlockSpec(memory_space=pltpu.VMEM),
            scratch_shapes=[
                pltpu.VMEM((slots, tile, cols), dtype),
                pltpu.VMEM((slots, channels * half, cols), dtype),
                pltpu.VMEM((slots, channels, tile, cols), dtype),
                pltpu.VMEM((2, half * GROUP, 128), jnp.float32),
                pltpu.SemaphoreType.DMA((slots,)),
                pltpu.SemaphoreType.DMA((slots,)),
            ],
        ),
        out_shape=jax.ShapeDtypeStruct((half, slots, cols), dtype),
        compiler_params=pltpu.CompilerParams(vmem_limit_bytes=58 << 20),
        cost_estimate=pl.CostEstimate(flops=flops, bytes_accessed=moved, transcendentals=0),
        name="transfer_and_apply",
    )(anchor, dims, pairs, core, got, other, right)


def on_device(sector_dims, new_owner, new_slot, block_pairs, theta_blocks, left_env, right_env):
    peers = lax.axis_size("sec")
    slots, channels, tile, _ = left_env.shape
    me = lax.axis_index("sec")
    core = lax.axis_index("mpo")
    core_word = core.astype(jnp.int32).reshape(1)

    tables = jnp.concatenate(
        [new_owner[None], new_slot[None], sector_dims[None], block_pairs.T], axis=0
    )
    tables = lax.all_gather(tables, ("sec", "mpo"), axis=0, tiled=False)
    right_other = lax.ppermute(right_env, "mpo", SWAP)

    parcels = pack(new_owner, core_word, theta_blocks, left_env, peers)
    got = lax.all_to_all(parcels, ("sec", "mpo"), split_axis=0, concat_axis=0, tiled=True)
    got, tables, right_other = lax.optimization_barrier((got, tables, right_other))
    bulk = channels * tile // 2
    other = lax.ppermute(got[:, bulk:], "mpo", SWAP)

    tables = tables.reshape(peers, 2, 3 + channels, slots)
    owner, slot, live = tables[:, 0, 0], tables[:, 0, 1], tables[:, 0, 2]
    lands = (owner == me)[:, :, None] & (
        slot[:, :, None] == jnp.arange(slots, dtype=jnp.int32)[None, None, :]
    )
    source = jnp.arange(peers, dtype=jnp.int32)[:, None, None]
    anchor = jnp.sum(jnp.where(lands, source, 0), axis=(0, 1))
    dims = jnp.sum(jnp.where(lands, live[:, :, None], 0), axis=(0, 1))
    pairs = lax.dynamic_index_in_dim(tables, me, 0, keepdims=False)[:, 3:].reshape(
        2 * channels, slots
    )
    first_right = jnp.where(core == 0, right_env, right_other)
    second_right = jnp.where(core == 0, right_other, right_env)
    right = jnp.concatenate([first_right, second_right], axis=0)
    return apply(anchor, dims, pairs, core_word, got, other, right, theta_blocks.dtype)


def solution(mesh):
    return jax.shard_map(
        on_device,
        mesh=mesh,
        in_specs=(
            P("sec"),
            P("sec"),
            P("sec"),
            P("sec", "mpo"),
            P("sec", None, None),
            P("sec", "mpo", None, None),
            P("mpo", None, None),
        ),
        out_specs=P("mpo", "sec", None),
        check_vma=False,
    )
```

time: 494 us -> 876 us (1.77)
  Pallas kernels: 0 us -> 512 us
  blocking collectives: 0 us -> 335 us
  waiting for transfers between devices: 317 us -> 4.01 us
  local copies, waits for them, and re-layouts: 56.5 us -> 5.75 us
  other arithmetic: 48.4 us -> 2.17 us
  matrix products: 24.3 us -> 0 us
  starting transfers between devices: 32.8 us -> 11.9 us
  between operations: 13.5 us -> 0.11 us
    pallas_call x0 -> x2, Pallas kernels: none -> 512 us  [the longest x1 479 us: pack(): pl.pallas_call(pack_kernel, grid_spec=pltpu.PrefetchScalarGridSpec(num_sc...]
    all_gather x0 -> x1, blocking collectives: none -> 335 us  [on_device(): tables = lax.all_gather(tables, ('sec', 'mpo'), axis=0, tiled=False)]
    all_to_all x3 -> x1, waiting for transfers between devices: 266 us -> 0.01 us  [on_device(): lax.all_to_all(parcels, ('sec', 'mpo'), split_axis=0, concat_axis=0, tile...]
    gather x5 -> x0, local copies, waits for them, and re-layouts: 52.6 us -> none  [the longest x2 20.6 us: arrange(): return jnp.take(received, anchor, axis=0)]
    reduce_scatter x1 -> x0, waiting for transfers between devices: 51 us -> none  [on_device(): lax.psum_scatter(jnp.einsum('swrc,swcn->rsn', left_new, partner, preferre...]
    select_n x7 -> x1, other arithmetic: 40.5 us -> 0.04 us  [on_device(): first_right = jnp.where(core == 0, right_env, right_other)]
    dot_general x2 -> x0, matrix products: 24.3 us -> none  [the longest x1 15.1 us: on_device(): jnp.einsum('swrc,swcn->rsn', left_new, partner, preferred_element_type=jn...]
    all_to_all x3 -> x1, starting transfers between devices: 32.6 us -> 11.1 us  [on_device(): lax.all_to_all(parcels, ('sec', 'mpo'), split_axis=0, concat_axis=0, tile...]
  transfers between devices with their start and end apart: 4 -> 3, of which waited for: 3 -> 1; matrix products, arithmetic and copies ran while one was open for 19% -> 0% of each run, Pallas kernels for 0% -> 0%
where the time goes in v1:
time: 876 us; the launch traced here: 871 us
  Pallas kernels  512 us (58%)
  blocking collectives  335 us (38%)
  starting transfers between devices  11.9 us (1%)
    pallas_call x1, Pallas kernels, pack(): pl.pallas_call(pack_kernel, grid_spec=pltpu.PrefetchScalarGridSpec(num_sc...  479 us
    all_gather x1, blocking collectives, on_device(): tables = lax.all_gather(tables, ('sec', 'mpo'), axis=0, tiled=False)  335 us
    pallas_call x1, Pallas kernels, apply(): pl.pallas_call(apply_kernel, grid_spec=pltpu.PrefetchScalarGridSpec(num_s...  33.7 us
  transfers between devices with their start and end apart: 3, of which 1 were waited for; matrix products, arithmetic and copies ran while one was open for 0% of the time, Pallas kernels for 0%

profile of v1, /device:TPU:11, one launch (start us, length us, event | category | flops | bytes accessed | tf_op | source)
XLA Modules:
  0.0 871.0 jit_solution(1073389644221762687)
XLA Ops:
  0.0 478.7 %pack_parcels.1 = bf16[128,320,256]{2,1,0:T(8,128)(2,1)} custom-call(s32[48]{0:T(128)} %owner_ref.1, s32[1]{0:T(128)} %bitcast.core_ref, bf16[48,256,256]{2,1,0:T(8,128)(2,1)} %theta_ref.1, bf16[48,2,256,256]{3,2,1,0:T(8,128)(2,1)} %left_ref.1), custom_call_target="tpu_custom_call" | custom-call | bytes 31457280 | tf_op jit(solution)/shard_map/pack_parcels/pallas_call | solution.py:51
  478.7 0.0 copy-start
  478.7 0.0 copy-start.1
  478.7 0.0 copy-start.2
  478.7 0.0 copy-start.3
  478.7 0.0 copy-start.4
  478.7 11.1 %all-to-all-start = ((bf16[128,320,256]{2,1,0:T(8,128)(2,1)}), bf16[128,320,256]{2,1,0:T(8,128)(2,1)}, u32[]{:S(2)}, u32[]{:S(2)}) async-start(bf16[128,320,256]{2,1,0:T(8,128)(2,1)} %pack_parcels.1), calls=%async_computation | async-start | bytes 41943040 | tf_op jit(solution)/shard_map/all_to_all | solution.py:195
  489.9 0.0 copy-done
  489.9 0.4 collective-permute-start
  490.3 0.0 copy-done.1
  490.3 0.0 copy-done.2
  490.3 0.0 copy-done.3
  490.3 0.0 copy-done.4
  490.4 334.7 %all-gather.1 = s32[128,5,48]{2,1,0:T(8,128)S(1)} all-gather(s32[1,5,48]{2,1,0:T(8,128)S(1)} %add_bitcast_fusion), channel_id=2, replica_groups=mesh['sec'=64,'mpo'=2] {'sec','mpo'}, dimensions={0}, use_global_device_ids=true | all-gather | bytes 123840 | tf_op jit(solution)/shard_map/all_gather | solution.py:191
  825.0 0.0 collective-permute-done
  825.0 0.0 all-to-all-done.got_ref
  825.1 4.8 slice.19
  829.8 0.4 collective-permute-start.1
  830.2 0.1 copy.24
  830.2 0.1 fusion.1
  830.3 0.1 copy.29
  830.4 0.1 copy.26
  830.5 0.1 copy.27
  830.6 0.6 copy.28
  831.2 0.9 pad_maximum_fusion.right_ref
  832.1 1.2 select_reduce_fusion
  833.3 4.0 collective-permute-done.1.other_ref
  837.3 33.7 %transfer_and_apply.1 = bf16[128,48,256]{2,1,0:T(8,128)(2,1)} custom-call(s32[48]{0:T(128)} %get-tuple-element.12.anchor_ref, s32[48]{0:T(128)} %get-tuple-element.11.dims_ref, s32[4,48]{1,0:T(4,128)} %bitcast.20, s32[1]{0:T(128)} %bitcast.core_ref, bf16[128,320,256]{2,1,0:T(8,128)(2,1)} %all-to-all-done.got_ref, ...), custom_call_target="tpu_custom_call" | custom-call | flops 9663676416 | bytes 22020096 | tf_op jit(solution)/shard_map/transfer_and_apply/pallas_call | solution.py:154
  (5 shorter events, 0.1 us)
Async XLA Ops:
  478.7 11.2 %copy-start = (bf16[2,256,256]{2,1,0:T(8,128)(2,1)S(1)}, bf16[2,256,256]{2,1,0:T(8,128)(2,1)}, u32[]{:S(2)}) copy-start(bf16[2,256,256]{2,1,0:T(8,128)(2,1)} %param.13) | copy-start | bytes 786436
  478.7 11.6 %copy-start.1 = (s32[48]{0:T(128)S(1)}, s32[48]{0:T(128)}, u32[]{:S(2)}) copy-start(s32[48]{0:T(128)} %owner_ref.1) | copy-start | bytes 580
  478.7 11.6 %copy-start.2 = (s32[48,2]{0,1:T(2,128)S(1)}, s32[48,2]{0,1:T(2,128)}, u32[]{:S(2)}) copy-start(s32[48,2]{0,1:T(2,128)} %param.10) | copy-start | bytes 1156
  478.7 11.6 %copy-start.3 = (s32[48]{0:T(128)S(1)}, s32[48]{0:T(128)}, u32[]{:S(2)}) copy-start(s32[48]{0:T(128)} %param.7) | copy-start | bytes 580
  478.7 11.6 %copy-start.4 = (s32[48]{0:T(128)S(1)}, s32[48]{0:T(128)}, u32[]{:S(2)}) copy-start(s32[48]{0:T(128)} %param.9) | copy-start | bytes 580
  478.7 346.3 %all-to-all-start = ((bf16[128,320,256]{2,1,0:T(8,128)(2,1)}), bf16[128,320,256]{2,1,0:T(8,128)(2,1)}, u32[]{:S(2)}, u32[]{:S(2)}) async-start(bf16[128,320,256]{2,1,0:T(8,128)(2,1)} %pack_parcels.1), calls=%async_computation | async-start | bytes 41943040 | tf_op jit(solution)/shard_map/all_to_all | solution.py:195
  489.9 335.2 %collective-permute-start = (bf16[2,256,256]{2,1,0:T(8,128)(2,1)S(1)}, bf16[2,256,256]{2,1,0:T(8,128)(2,1)S(1)}, u32[]{:S(2)}, u32[]{:S(2)}) collective-permute-start(bf16[2,256,256]{2,1,0:T(8,128)(2,1)S(1)} %copy-done), channel_id=1, source_target_pairs={{0,1},{1,0},{2,3},{3,2},{4,5},{5,4},{6,7},{7,6},{8,9},{9,8},{10,11... | collective-permute-start | bytes 786440 | tf_op jit(solution)/shard_map/ppermute | solution.py:192
  829.8 7.5 collective-permute-start.1

commit v2 on v1

--- a/solution.py
+++ b/solution.py
@@ -9,58 +9,94 @@
 
 SWAP = [(0, 1), (1, 0)]
 GROUP = 16
-
-
-def pack_kernel(owner_ref, core_ref, theta_ref, left_ref, out_ref, sems):
-    slots, channels, tile, _ = left_ref.shape
+TAIL = 8
+
+
+def pack_kernel(
+    owner_ref, slot_ref, dims_ref, core_ref, theta_ref, left_ref, out_ref,
+    staged, blank, load_sems, store_sems, blank_sem,
+):
+    slots, channels, tile, cols = left_ref.shape
     half, quarter = tile // 2, tile // 4
+    bulk = channels * half
     core = core_ref[0]
 
-    def send(i, carry):
-        owner = owner_ref[i]
+    def load(i, carry):
         for h in range(2):
-            place = 2 * owner + h
             for w in range(channels):
                 pltpu.make_async_copy(
                     left_ref.at[i, w, pl.ds(h * half, half)],
-                    out_ref.at[place, pl.ds(w * half, half)],
-                    sems.at[i],
+                    staged.at[i, h, pl.ds(w * half, half)],
+                    load_sems.at[i],
                 ).start()
             first = pl.multiple_of(h * half + core * quarter, quarter)
             pltpu.make_async_copy(
                 theta_ref.at[i, pl.ds(first, quarter)],
-                out_ref.at[place, pl.ds(channels * half, quarter)],
-                sems.at[i],
-            ).start()
-        return carry
-
-    lax.fori_loop(0, slots, send, 0)
+                staged.at[i, h, pl.ds(bulk, quarter)],
+                load_sems.at[i],
+            ).start()
+        return carry
+
+    lax.fori_loop(0, slots, load, 0)
+
+    blank[...] = jnp.zeros_like(blank)
+    clear = pltpu.make_async_copy(
+        blank, out_ref.at[:, pl.ds(bulk + quarter, TAIL)], blank_sem
+    )
+    clear.start()
+    clear.wait()
+    tail_rows = lax.broadcasted_iota(jnp.int32, (TAIL, cols), 0)
+
+    def store(i, carry):
+        note = jnp.where(tail_rows == 0, slot_ref[i] + 1, dims_ref[i])
+        note = note.astype(jnp.float32).astype(staged.dtype)
+        for h in range(2):
+            staged[i, h, bulk + quarter:] = note
+        body = staged.at[i, :, pl.ds(0, bulk + quarter)]
+        pltpu.make_async_copy(body, body, load_sems.at[i]).wait()
+        place = 2 * owner_ref[i]
+        pltpu.make_async_copy(
+            staged.at[i], out_ref.at[pl.ds(place, 2)], store_sems.at[i]
+        ).start()
+        return carry
+
+    lax.fori_loop(0, slots, store, 0)
 
     def settle(i, carry):
-        pair = out_ref.at[pl.ds(2 * owner_ref[i], 2)]
-        pltpu.make_async_copy(pair, pair, sems.at[i]).wait()
+        place = 2 * owner_ref[i]
+        pltpu.make_async_copy(
+            staged.at[i], out_ref.at[pl.ds(place, 2)], store_sems.at[i]
+        ).wait()
         return carry
 
     lax.fori_loop(0, slots, settle, 0)
 
 
-def pack(new_owner, core, theta_blocks, left_env, peers):
+def pack(new_owner, new_slot, sector_dims, core, theta_blocks, left_env, peers):
     slots, channels, tile, cols = left_env.shape
-    rows = channels * tile // 2 + tile // 4
+    rows = channels * tile // 2 + tile // 4 + TAIL
+    dtype = theta_blocks.dtype
     moved = 2 * slots * 2 * rows * cols * 2
     return pl.pallas_call(
         pack_kernel,
         grid_spec=pltpu.PrefetchScalarGridSpec(
-            num_scalar_prefetch=2,
+            num_scalar_prefetch=4,
             grid=(),
             in_specs=[pl.BlockSpec(memory_space=pltpu.HBM)] * 2,
             out_specs=pl.BlockSpec(memory_space=pltpu.HBM),
-            scratch_shapes=[pltpu.SemaphoreType.DMA((slots,))],
+            scratch_shapes=[
+                pltpu.VMEM((slots, 2, rows, cols), dtype),
+                pltpu.VMEM((2 * peers, TAIL, cols), dtype),
+                pltpu.SemaphoreType.DMA((slots,)),
+                pltpu.SemaphoreType.DMA((slots,)),
+                pltpu.SemaphoreType.DMA,
+            ],
         ),
-        out_shape=jax.ShapeDtypeStruct((2 * peers, rows, cols), theta_blocks.dtype),
+        out_shape=jax.ShapeDtypeStruct((2 * peers, rows, cols), dtype),
+        compiler_params=pltpu.CompilerParams(vmem_limit_bytes=40 << 20),
         cost_estimate=pl.CostEstimate(flops=0, bytes_accessed=moved, transcendentals=0),
         name="pack_parcels",
-    )(new_owner, core, theta_blocks, left_env)
+    )(new_owner, new_slot, sector_dims, core, theta_blocks, left_env)
 
 
 def apply_kernel(
@@ -72,7 +108,7 @@
     channels = right_ref.shape[0]
     half, quarter = tile // 2, tile // 4
     core = core_ref[0]
-    bulk = got_ref.shape[1] - quarter
+    bulk = got_ref.shape[1] - quarter - TAIL
 
     def fetch_theta(j, carry):
         source = anchor_ref[j]
@@ -181,36 +217,40 @@
 def on_device(sector_dims, new_owner, new_slot, block_pairs, theta_blocks, left_env, right_env):
     peers = lax.axis_size("sec")
     slots, channels, tile, _ = left_env.shape
-    me = lax.axis_index("sec")
     core = lax.axis_index("mpo")
     core_word = core.astype(jnp.int32).reshape(1)
 
-    tables = jnp.concatenate(
-        [new_owner[None], new_slot[None], sector_dims[None], block_pairs.T], axis=0
-    )
-    tables = lax.all_gather(tables, ("sec", "mpo"), axis=0, tiled=False)
     right_other = lax.ppermute(right_env, "mpo", SWAP)
-
-    parcels = pack(new_owner, core_word, theta_blocks, left_env, peers)
+    pairs_other = lax.ppermute(block_pairs, "mpo", SWAP)
+    parcels = pack(
+        new_owner, new_slot, sector_dims, core_word, theta_blocks, left_env, peers
+    )
+    parcels, right_other, pairs_other = lax.optimization_barrier(
+        (parcels, right_other, pairs_other)
+    )
     got = lax.all_to_all(parcels, ("sec", "mpo"), split_axis=0, concat_axis=0, tiled=True)
-    got, tables, right_other = lax.optimization_barrier((got, tables, right_other))
+    got, right_other, pairs_other, core = lax.optimization_barrier(
+        (got, right_other, pairs_other, core)
+    )
     bulk = channels * tile // 2
-    other = lax.ppermute(got[:, bulk:], "mpo", SWAP)
-
-    tables = tables.reshape(peers, 2, 3 + channels, slots)
-    owner, slot, live = tables[:, 0, 0], tables[:, 0, 1], tables[:, 0, 2]
-    lands = (owner == me)[:, :, None] & (
-        slot[:, :, None] == jnp.arange(slots, dtype=jnp.int32)[None, None, :]
-    )
-    source = jnp.arange(peers, dtype=jnp.int32)[:, None, None]
-    anchor = jnp.sum(jnp.where(lands, source, 0), axis=(0, 1))
-    dims = jnp.sum(jnp.where(lands, live[:, :, None], 0), axis=(0, 1))
-    pairs = lax.dynamic_index_in_dim(tables, me, 0, keepdims=False)[:, 3:].reshape(
-        2 * channels, slots
-    )
-    first_right = jnp.where(core == 0, right_env, right_other)
-    second_right = jnp.where(core == 0, right_other, right_env)
-    right = jnp.concatenate([first_right, second_right], axis=0)
+    notes = bulk + tile // 4
+    other = lax.ppermute(got[:, bulk:notes], "mpo", SWAP)
+
+    slot = got[0::2, notes, 0].astype(jnp.int32)
+    live = got[0::2, notes + 1, 0].astype(jnp.int32)
+    lands = slot[None, :] == jnp.arange(1, slots + 1, dtype=jnp.int32)[:, None]
+    source = jnp.arange(peers, dtype=jnp.int32)[None, :]
+    anchor = jnp.sum(jnp.where(lands, source, 0), axis=1)
+    dims = jnp.sum(jnp.where(lands, live[None, :], 0), axis=1)
+    first = core == 0
+    pairs = jnp.concatenate(
+        [jnp.where(first, block_pairs, pairs_other), jnp.where(first, pairs_other, block_pairs)],
+        axis=1,
+    ).T
+    right = jnp.concatenate(
+        [jnp.where(first, right_env, right_other), jnp.where(first, right_other, right_env)],
+        axis=0,
+    )
     return apply(anchor, dims, pairs, core_word, got, other, right, theta_blocks.dtype)
 
 

time: 876 us -> 325 us (0.37)
  Pallas kernels: 512 us -> 46.4 us
  blocking collectives: 335 us -> 255 us
  starting transfers between devices: 11.9 us -> 1.07 us
    pallas_call x1, Pallas kernels: 479 us -> 12.7 us  [pack(): pl.pallas_call(pack_kernel, grid_spec=pltpu.PrefetchScalarGridSpec(num_sc...]
    all_gather x1 -> x0, blocking collectives: 335 us -> none  [on_device(): tables = lax.all_gather(tables, ('sec', 'mpo'), axis=0, tiled=False)]
    all_to_all x0 -> x1, blocking collectives: none -> 255 us  [on_device(): lax.all_to_all(parcels, ('sec', 'mpo'), split_axis=0, concat_axis=0, tile...]
    unnamed x11 -> x14, local copies, waits for them, and re-layouts: 0.1 us -> 11.9 us
    all_to_all x1 -> x0, starting transfers between devices: 11.1 us -> none  [on_device(): lax.all_to_all(parcels, ('sec', 'mpo'), split_axis=0, concat_axis=0, tile...]
  transfers between devices with their start and end apart: 3 -> 3, of which waited for: 1 -> 1; matrix products, arithmetic and copies ran while one was open for 0% -> 2% of each run, Pallas kernels for 0% -> 4%
where the time goes in v2:
time: 325 us
  blocking collectives  255 us (78%)
  Pallas kernels  46.4 us (14%)
  local copies, waits for them, and re-layouts  14.5 us (4%)
  other arithmetic  5.56 us (2%)
    all_to_all x1, blocking collectives, on_device(): lax.all_to_all(parcels, ('sec', 'mpo'), split_axis=0, concat_axis=0, tile...  255 us
    pallas_call x1, Pallas kernels, apply(): pl.pallas_call(apply_kernel, grid_spec=pltpu.PrefetchScalarGridSpec(num_s...  33.6 us
    pallas_call x1, Pallas kernels, pack(): pl.pallas_call(pack_kernel, grid_spec=pltpu.PrefetchScalarGridSpec(num_sc...  12.7 us
    unnamed x14, local copies, waits for them, and re-layouts  11.9 us
  transfers between devices with their start and end apart: 3, of which 1 were waited for; matrix products, arithmetic and copies ran while one was open for 2% of the time, Pallas kernels for 4%

profile of v2, /device:TPU:11, one launch (start us, length us, event | category | flops | bytes accessed | tf_op | source)
XLA Modules:
  0.0 324.5 jit_solution(14010333209968009798)
XLA Ops:
  0.0 0.7 collective-permute-start
  0.7 0.0 collective-permute-start.1
  0.7 0.0 copy-start
  0.7 2.8 copy-done
  3.5 0.0 copy-start.1
  3.5 0.7 copy-done.1
  4.1 0.0 copy-start.2
  4.1 0.7 copy-done.2
  4.8 0.0 copy-start.3
  4.8 0.7 copy-done.3
  5.4 12.7 %pack_parcels.1 = bf16[128,328,256]{2,1,0:T(8,128)(2,1)} custom-call(s32[48]{0:T(128)S(1)} %copy-done.1, s32[48]{0:T(128)S(1)} %copy-done.2, s32[48]{0:T(128)S(1)} %copy-done.3, s32[1]{0:T(128)} %bitcast.core_ref, bf16[48,256,256]{2,1,0:T(8,128)(2,1)S(1)} %copy-done, bf16[48,2,256,256]{3,2,1,0:T(8,128)(2,1)} %left_ref.1), custom_call_target="tpu_custom_call" | custom-call | bytes 32243712 | tf_op jit(solution)/shard_map/pack_parcels/pallas_call | solution.py:80
  18.2 0.0 copy-start.6
  18.2 0.0 copy-start.5
  18.2 0.0 collective-permute-done.1
  18.2 0.0 collective-permute-done
  18.2 255.4 %all_to_all.5.got_ref = bf16[128,328,256]{2,1,0:T(8,128)(2,1)S(1)} all-to-all(bf16[128,328,256]{2,1,0:T(8,128)(2,1)} %pack_parcels.1), channel_id=1, replica_groups=mesh['sec'=64,'mpo'=2] {'sec','mpo'}, dimensions={0} | all-to-all | bytes 42991616 | tf_op jit(solution)/shard_map/all_to_all | solution.py:231
  273.6 0.0 copy-start.4
  273.6 7.2 %copy-done.4 = bf16[128,328,256]{2,1,0:T(8,128)(2,1)} copy-done((bf16[128,328,256]{2,1,0:T(8,128)(2,1)}, bf16[128,328,256]{2,1,0:T(8,128)(2,1)S(1)}, u32[]{:S(2)}) %copy-start.4) | copy-done | bytes 21495832
  280.8 2.6 slice.11
  283.4 0.4 collective-permute-start.2
  283.8 0.0 copy-done.6
  283.8 0.6 add_bitcast_fusion.pairs_ref
  284.3 3.3 %convert_reduce_fusion = (s32[64]{0:T(128)S(1)}, s32[64]{0:T(128)S(1)}) fusion(bf16[128,328,256]{2,1,0:T(8,128)(2,1)} %copy-done.4), kind=kLoop, calls=%fused_computation.3 | loop fusion | flops 128 | bytes 768 | tf_op jit(solution)/shard_map/convert_element_type | solution.py:240
  287.7 0.7 fusion.1
  288.4 0.0 copy-done.5
  288.5 0.9 pad_maximum_fusion.right_ref
  289.3 1.6 collective-permute-done.2.other_ref
  290.9 33.6 %transfer_and_apply.1 = bf16[128,48,256]{2,1,0:T(8,128)(2,1)} custom-call(s32[48]{0:T(128)} %get-tuple-element.22.anchor_ref, s32[48]{0:T(128)} %get-tuple-element.21.dims_ref, s32[4,48]{1,0:T(4,128)} %add_bitcast_fusion.pairs_ref, s32[1]{0:T(128)} %bitcast.core_ref, bf16[128,328,256]{2,1,0:T(8,128)(2,1)} %copy-done.4, ...), custom_call_target="tpu_custom_call" | custom-call | flops 9663676416 | bytes 22020096 | tf_op jit(solution)/shard_map/transfer_and_apply/pallas_call | solution.py:190
  (3 shorter events, 0.0 us)
Async XLA Ops:
  0.0 18.2 %collective-permute-start = (bf16[2,256,256]{2,1,0:T(8,128)(2,1)}, bf16[2,256,256]{2,1,0:T(8,128)(2,1)S(1)}, u32[]{:S(2)}, u32[]{:S(2)}) collective-permute-start(bf16[2,256,256]{2,1,0:T(8,128)(2,1)} %param.13), channel_id=1, source_target_pairs={{0,1},{1,0},{2,3},{3,2},{4,5},{5,4},{6,7},{7,6},{8,9},{9,8},{10,11... | collective-permute-start | bytes 786440 | tf_op jit(solution)/shard_map/ppermute | solution.py:223
  0.7 17.5 %collective-permute-start.1 = (s32[48,2]{0,1:T(2,128)}, s32[48,2]{0,1:T(2,128)S(1)}, u32[]{:S(2)}, u32[]{:S(2)}) collective-permute-start(s32[48,2]{0,1:T(2,128)} %param.10), channel_id=1, source_target_pairs={{0,1},{1,0},{2,3},{3,2},{4,5},{5,4},{6,7},{7,6},{8,9},{9,8},{10,11... | collective-permute-start | bytes 1160 | tf_op jit(solution)/shard_map/ppermute | solution.py:224
  0.7 2.8 copy-start
  3.5 0.7 copy-start.1
  4.1 0.7 copy-start.2
  4.8 0.7 copy-start.3
  18.2 265.6 %copy-start.6 = (s32[48,2]{0,1:T(2,128)S(1)}, s32[48,2]{0,1:T(2,128)}, u32[]{:S(2)}) copy-start(s32[48,2]{0,1:T(2,128)} %param.10) | copy-start | bytes 1156
  18.2 270.2 %copy-start.5 = (bf16[2,256,256]{2,1,0:T(8,128)(2,1)S(1)}, bf16[2,256,256]{2,1,0:T(8,128)(2,1)}, u32[]{:S(2)}) copy-start(bf16[2,256,256]{2,1,0:T(8,128)(2,1)} %param.13) | copy-start | bytes 786436
  273.6 7.2 %copy-start.4 = (bf16[128,328,256]{2,1,0:T(8,128)(2,1)}, bf16[128,328,256]{2,1,0:T(8,128)(2,1)S(1)}, u32[]{:S(2)}) copy-start(bf16[128,328,256]{2,1,0:T(8,128)(2,1)S(1)} %all_to_all.5.got_ref) | copy-start | bytes 64487428
  283.4 7.5 %collective-permute-start.2 = (bf16[128,64,256]{2,1,0:T(8,128)(2,1)}, bf16[128,64,256]{2,1,0:T(8,128)(2,1)}, u32[]{:S(2)}, u32[]{:S(2)}) collective-permute-start(bf16[128,64,256]{2,1,0:T(8,128)(2,1)} %slice.11), channel_id=1, source_target_pairs={{0,1},{1,0},{2,3},{3,2},{4,5},{5,4},{6,7},{7,6},{8,9},{9,8},{10,11... | collective-permute-start | bytes 12582920 | tf_op jit(solution)/shard_map/ppermute | solution.py:237

commit v3 on v2

v3 whole, which is shorter than its diff:
```python
import jax
import jax.numpy as jnp
from jax import lax
from jax.experimental import pallas as pl
from jax.experimental.pallas import tpu as pltpu
from jax.sharding import PartitionSpec as P

SWAP = [(0, 1), (1, 0)]
TAIL = 8
GROUP = 16
STEP = 4
LANES = 128
HBM = pl.BlockSpec(memory_space=pltpu.HBM)


def copy(source, target, sem):
    return pltpu.make_async_copy(source, target, sem)


def pack_kernel(
    owner_ref, slot_ref, dims_ref, core_ref, theta_ref, left_ref, out_ref,
    staged, blank, load_sems, store_sems, blank_sem,
):
    slots, channels, _, half, cols = left_ref.shape
    quarter = half // 2
    bulk = channels * half
    core = core_ref[0]

    def load(i, carry):
        for h in range(2):
            copy(
                left_ref.at[i, :, h],
                staged.at[i, h, pl.ds(0, bulk)].reshape(channels, half, cols),
                load_sems.at[i],
            ).start()
        copy(
            theta_ref.at[i, :, core],
            staged.at[i, :, pl.ds(bulk, quarter)],
            load_sems.at[i],
        ).start()
        return carry

    lax.fori_loop(0, slots, load, 0)

    blank[...] = jnp.zeros_like(blank)
    clear = copy(blank, out_ref.at[:, pl.ds(bulk + quarter, TAIL)], blank_sem)
    clear.start()
    clear.wait()
    tail_rows = lax.broadcasted_iota(jnp.int32, (TAIL, cols), 0)

    def store(i, carry):
        note = jnp.where(tail_rows == 0, slot_ref[i] + 1, dims_ref[i])
        note = note.astype(jnp.float32).astype(staged.dtype)
        for h in range(2):
            staged[i, h, bulk + quarter:] = note
        body = staged.at[i, :, pl.ds(0, bulk + quarter)]
        copy(body, body, load_sems.at[i]).wait()
        place = 2 * owner_ref[i]
        copy(staged.at[i], out_ref.at[pl.ds(place, 2)], store_sems.at[i]).start()
        return carry

    lax.fori_loop(0, slots, store, 0)

    def settle(i, carry):
        place = 2 * owner_ref[i]
        copy(staged.at[i], out_ref.at[pl.ds(place, 2)], store_sems.at[i]).wait()
        return carry

    lax.fori_loop(0, slots, settle, 0)


def pack(new_owner, new_slot, sector_dims, core, theta_blocks, left_env, peers):
    slots, channels, tile, cols = left_env.shape
    half, quarter = tile // 2, tile // 4
    rows = channels * half + quarter + TAIL
    dtype = theta_blocks.dtype
    moved = 2 * slots * 2 * rows * cols * 2
    return pl.pallas_call(
        pack_kernel,
        grid_spec=pltpu.PrefetchScalarGridSpec(
            num_scalar_prefetch=4,
            grid=(),
            in_specs=[HBM] * 2,
            out_specs=HBM,
            scratch_shapes=[
                pltpu.VMEM((slots, 2, rows, cols), dtype),
                pltpu.VMEM((2 * peers, TAIL, cols), dtype),
                pltpu.SemaphoreType.DMA((slots,)),
                pltpu.SemaphoreType.DMA((slots,)),
                pltpu.SemaphoreType.DMA,
            ],
        ),
        out_shape=jax.ShapeDtypeStruct((2 * peers, rows, cols), dtype),
        compiler_params=pltpu.CompilerParams(vmem_limit_bytes=60 << 20),
        cost_estimate=pl.CostEstimate(flops=0, bytes_accessed=moved, transcendentals=0),
        name="pack_parcels",
    )(
        new_owner, new_slot, sector_dims, core,
        theta_blocks.reshape(slots, 2, 2, quarter, cols),
        left_env.reshape(slots, channels, 2, half, cols),
    )


def split_kernel(got_ref, quarters_ref, places_ref, notes, quarter_sem, note_sem):
    parcels, quarter, _ = quarters_ref.shape
    end = got_ref.shape[1]
    theta = copy(
        got_ref.at[:, pl.ds(end - TAIL - quarter, quarter)], quarters_ref, quarter_sem
    )
    tails = copy(
        got_ref.at[:, pl.ds(end - TAIL, TAIL), pl.ds(0, LANES)], notes, note_sem
    )
    tails.start()
    theta.start()
    tails.wait()
    tail = notes[...].astype(jnp.float32)
    row = lax.broadcasted_iota(jnp.int32, tail.shape, 1)
    slot = jnp.sum(jnp.where(row == 0, tail, 0.0), axis=1)
    live = jnp.sum(jnp.where(row == 1, tail, 0.0), axis=1)
    parcel = lax.broadcasted_iota(jnp.int32, slot.shape, 0)
    wanted = lax.broadcasted_iota(jnp.int32, slot.shape, 1) + 1
    lands = (slot.astype(jnp.int32) == wanted) & (parcel % 2 == 0)
    anchor = jnp.sum(jnp.where(lands, parcel, 0), axis=0, keepdims=True)
    dims = jnp.sum(jnp.where(lands, live.astype(jnp.int32), 0), axis=0, keepdims=True)
    places_ref[0:1, :] = anchor
    places_ref[1:2, :] = dims
    theta.wait()


def split(got, quarter):
    parcels, rows, cols = got.shape
    return pl.pallas_call(
        split_kernel,
        in_specs=[HBM],
        out_specs=[pl.BlockSpec(memory_space=pltpu.VMEM)] * 2,
        scratch_shapes=[
            pltpu.VMEM((parcels, TAIL, LANES), got.dtype),
            pltpu.SemaphoreType.DMA,
            pltpu.SemaphoreType.DMA,
        ],
        out_shape=[
            jax.ShapeDtypeStruct((parcels, quarter, cols), got.dtype),
            jax.ShapeDtypeStruct((2, LANES), jnp.int32),
        ],
        compiler_params=pltpu.CompilerParams(vmem_limit_bytes=60 << 20),
        name="split_parcels",
    )(got)


def apply_kernel(
    places_ref, pairs_ref, core_ref, got_ref, other_ref, right_ref, out_ref,
    theta, left, inner, rows_f32, theta_sems, left_sems,
):
    slots, _, _, quarter, cols = theta.shape
    channels = left.shape[1] * left.shape[2]
    half, tile = 2 * quarter, 4 * quarter
    bulk = channels * half // 2
    core = core_ref[0]

    def fetch_theta(j, carry):
        source = places_ref[0, j]
        copy(
            got_ref.at[pl.ds(source, 2), pl.ds(bulk, quarter)],
            theta.at[j, core],
            theta_sems.at[j],
        ).start()
        copy(other_ref.at[pl.ds(source, 2)], theta.at[j, 1 - core], theta_sems.at[j]).start()
        return carry

    def fetch_left(j, carry):
        source = places_ref[0, j]
        copy(
            got_ref.at[pl.ds(source, 2), pl.ds(0, bulk)],
            left.at[j].reshape(2, bulk, cols),
            left_sems.at[j],
        ).start()
        return carry

    lax.fori_loop(0, slots, fetch_theta, 0)
    lax.fori_loop(0, slots, fetch_left, 0)

    strip = 16
    strip_rows = lax.broadcasted_iota(jnp.int32, (strip, cols), 0)

    def trim(j, carry):
        copy(theta.at[j], theta.at[j], theta_sems.at[j]).wait()
        live = places_ref[1, j]
        block = theta.at[j].reshape(tile, cols)

        def clear(t, inner_carry):
            first = pl.multiple_of(t * strip, strip)
            rows = block[pl.ds(first, strip)].astype(jnp.float32)
            rows = jnp.where(strip_rows + first < live, rows, 0.0)
            block[pl.ds(first, strip)] = rows.astype(theta.dtype)
            return inner_carry

        return lax.fori_loop(live // strip, tile // strip, clear, carry)

    lax.fori_loop(0, slots, trim, 0)

    half_ids = lax.broadcasted_iota(jnp.int32, (half, cols), 0) + core * half

    for g in range(slots // GROUP):

        def contract(b, carry):
            for k in range(STEP):
                j = g * GROUP + b * STEP + k
                copy(left.at[j], left.at[j], left_sems.at[j]).wait()
                for w in range(channels):
                    partner = theta[pairs_ref[w, j]].reshape(tile, cols)
                    inner[k * half:(k + 1) * half, w * cols:(w + 1) * cols] = jnp.dot(
                        left[j, w // 2, w % 2],
                        partner,
                        preferred_element_type=jnp.float32,
                    ).astype(inner.dtype)
            total = jnp.dot(
                inner[...], right_ref[...], preferred_element_type=jnp.float32
            )
            for k in range(STEP):
                j = g * GROUP + b * STEP + k
                kept = jnp.where(
                    half_ids < places_ref[1, j], total[k * half:(k + 1) * half], 0.0
                )
                for side in range(2):
                    rows_f32[side, pl.ds(b * STEP + k, half, stride=GROUP)] = kept[
                        :, side * LANES:(side + 1) * LANES
                    ]
            return carry

        lax.fori_loop(0, GROUP // STEP, contract, 0)
        for side in range(2):
            out_ref[:, g * GROUP:(g + 1) * GROUP, side * LANES:(side + 1) * LANES] = (
                rows_f32[side].reshape(half, GROUP, LANES).astype(out_ref.dtype)
            )


def apply(places, pairs, core, got, other, right, dtype):
    channels, tile, cols = right.shape
    slots = pairs.shape[1]
    half, quarter = tile // 2, tile // 4
    flops = 4 * slots * channels * half * tile * cols
    moved = 2 * slots * cols * (tile + channels * half + half)
    return pl.pallas_call(
        apply_kernel,
        grid_spec=pltpu.PrefetchScalarGridSpec(
            num_scalar_prefetch=3,
            grid=(),
            in_specs=[HBM, HBM, pl.BlockSpec(memory_space=pltpu.VMEM)],
            out_specs=pl.BlockSpec(memory_space=pltpu.VMEM),
            scratch_shapes=[
                pltpu.VMEM((slots, 2, 2, quarter, cols), dtype),
                pltpu.VMEM((slots, 2, channels // 2, half, cols), dtype),
                pltpu.VMEM((STEP * half, channels * cols), dtype),
                pltpu.VMEM((2, half * GROUP, LANES), jnp.float32),
                pltpu.SemaphoreType.DMA((slots,)),
                pltpu.SemaphoreType.DMA((slots,)),
            ],
        ),
        out_shape=jax.ShapeDtypeStruct((half, slots, cols), dtype),
        compiler_params=pltpu.CompilerParams(vmem_limit_bytes=60 << 20),
        cost_estimate=pl.CostEstimate(flops=flops, bytes_accessed=moved, transcendentals=0),
        name="contract",
    )(places, pairs, core, got, other, right.reshape(channels * tile, cols))


def on_device(sector_dims, new_owner, new_slot, block_pairs, theta_blocks, left_env, right_env):
    peers = lax.axis_size("sec")
    core = lax.axis_index("mpo")
    core_word = core.astype(jnp.int32).reshape(1)

    right_other = lax.ppermute(right_env, "mpo", SWAP)
    pairs_other = lax.ppermute(block_pairs, "mpo", SWAP)
    parcels = pack(
        new_owner, new_slot, sector_dims, core_word, theta_blocks, left_env, peers
    )
    parcels, right_other, pairs_other = lax.optimization_barrier(
        (parcels, right_other, pairs_other)
    )
    got = lax.all_to_all(parcels, ("sec", "mpo"), split_axis=0, concat_axis=0, tiled=True)
    got, right_other, pairs_other, core = lax.optimization_barrier(
        (got, right_other, pairs_other, core)
    )
    quarters, places = split(got, theta_blocks.shape[1] // 4)
    other = lax.ppermute(quarters, "mpo", SWAP)
    first = core == 0
    pairs = jnp.concatenate(
        [jnp.where(first, block_pairs, pairs_other), jnp.where(first, pairs_other, block_pairs)],
        axis=1,
    ).T
    right = jnp.concatenate(
        [jnp.where(first, right_env, right_other), jnp.where(first, right_other, right_env)],
        axis=0,
    )
    return apply(places, pairs, core_word, got, other, right, theta_blocks.dtype)


def solution(mesh):
    return jax.shard_map(
        on_device,
        mesh=mesh,
        in_specs=(
            P("sec"),
            P("sec"),
            P("sec"),
            P("sec", "mpo"),
            P("sec", None, None),
            P("sec", "mpo", None, None),
            P("mpo", None, None),
        ),
        out_specs=P("mpo", "sec", None),
        check_vma=False,
    )
```

time: 325 us -> 305 us (0.938)
  local copies, waits for them, and re-layouts: 14.5 us -> 0.01 us
  Pallas kernels: 46.4 us -> 41.4 us
  waiting for transfers between devices: 1.56 us -> 5.67 us
  other arithmetic: 5.56 us -> 1.46 us
    unnamed x14 -> x4, local copies, waits for them, and re-layouts: 11.9 us -> 0.01 us
    pallas_call x1, Pallas kernels: 33.6 us -> 24.1 us  [apply(): pl.pallas_call(apply_kernel, grid_spec=pltpu.PrefetchScalarGridSpec(num_s...]
    pallas_call x0 -> x1, Pallas kernels: none -> 4.35 us  [split(): pl.pallas_call(split_kernel, in_specs=[HBM], out_specs=[pl.BlockSpec(memo...]
    ppermute x1, waiting for transfers between devices: 1.56 us -> 5.66 us  [on_device(): other = lax.ppermute(quarters, 'mpo', SWAP)]
    convert_element_type x1 -> x0, other arithmetic: 3.34 us -> none  [on_device(): live = got[0::2, notes + 1, 0].astype(jnp.int32)]
  transfers between devices with their start and end apart: 3 -> 3, of which waited for: 1 -> 1; matrix products, arithmetic and copies ran while one was open for 2% -> 0% of each run, Pallas kernels for 4% -> 4%
where the time goes in v3:
time: 305 us
  blocking collectives  255 us (84%)
  Pallas kernels  41.4 us (14%)
  waiting for transfers between devices  5.67 us (2%)
    all_to_all x1, blocking collectives, on_device(): lax.all_to_all(parcels, ('sec', 'mpo'), split_axis=0, concat_axis=0, tile...  255 us
    pallas_call x1, Pallas kernels, apply(): pl.pallas_call(apply_kernel, grid_spec=pltpu.PrefetchScalarGridSpec(num_s...  24.1 us
    pallas_call x1, Pallas kernels, pack(): pl.pallas_call(pack_kernel, grid_spec=pltpu.PrefetchScalarGridSpec(num_sc...  12.9 us
  transfers between devices with their start and end apart: 3, of which 1 were waited for; matrix products, arithmetic and copies ran while one was open for 0% of the time, Pallas kernels for 4%

profile of v3, /device:TPU:11, one launch (start us, length us, event | category | flops | bytes accessed | tf_op | source)
XLA Modules:
  0.0 305.1 jit_solution(4138877164969218379)
XLA Ops:
  0.0 0.7 collective-permute-start
  0.7 0.0 collective-permute-start.1
  0.7 12.9 %pack_parcels.1 = bf16[128,328,256]{2,1,0:T(8,128)(2,1)} custom-call(s32[48]{0:T(128)} %owner_ref.1, s32[48]{0:T(128)} %slot_ref.1, s32[48]{0:T(128)} %dims_ref.1, s32[1]{0:T(128)} %bitcast.core_ref, bf16[48,2,2,64,256]{4,3,2,1,0:T(8,128)(2,1)} %bitcast.7, bf16[48,2,2,128,256]{4,3,2,1,0:T(8,128)(2,1)} %bitcast.6), custom_call_target="tpu_custom_call" | custom-call | bytes 32243712 | tf_op jit(solution)/shard_map/pack_parcels/pallas_call | solution.py:78
  13.6 0.0 collective-permute-done.1
  13.6 0.0 collective-permute-done
  13.6 255.4 %all_to_all.5.got_ref = bf16[128,328,256]{2,1,0:T(8,128)(2,1)} all-to-all(bf16[128,328,256]{2,1,0:T(8,128)(2,1)} %pack_parcels.1), channel_id=1, replica_groups=mesh['sec'=64,'mpo'=2] {'sec','mpo'}, dimensions={0} | all-to-all | bytes 42991616 | tf_op jit(solution)/shard_map/all_to_all | solution.py:279
  269.0 0.0 copy-start.1
  269.0 0.0 copy-start
  269.0 4.3 %split_parcels.1 = (bf16[128,64,256]{2,1,0:T(8,128)(2,1)}, s32[2,128]{1,0:T(2,128)}) custom-call(bf16[128,328,256]{2,1,0:T(8,128)(2,1)} %all_to_all.5.got_ref), custom_call_target="tpu_custom_call" | custom-call | tf_op jit(solution)/shard_map/split_parcels/pallas_call | solution.py:132
  273.4 0.5 collective-permute-start.2
  273.9 0.0 copy-done.1
  273.9 0.5 add_bitcast_fusion.pairs_ref
  274.4 0.0 copy-done
  274.5 0.9 pad_maximum_fusion
  275.3 5.7 %collective-permute-done.2.other_ref = bf16[128,64,256]{2,1,0:T(8,128)(2,1)} collective-permute-done((bf16[128,64,256]{2,1,0:T(8,128)(2,1)}, bf16[128,64,256]{2,1,0:T(8,128)(2,1)}, u32[]{:S(2)}, u32[]{:S(2)}) %collective-permute-start.2) | collective-permute-done | bytes 4194336 | tf_op jit(solution)/shard_map/ppermute | solution.py:284
  281.0 24.1 %contract.1 = bf16[128,48,256]{2,1,0:T(8,128)(2,1)} custom-call(s32[2,128]{1,0:T(2,128)} %get-tuple-element.18.places_ref, s32[4,48]{1,0:T(4,128)} %add_bitcast_fusion.pairs_ref, s32[1]{0:T(128)} %bitcast.core_ref, bf16[128,328,256]{2,1,0:T(8,128)(2,1)} %all_to_all.5.got_ref, bf16[128,64,256]{2,1,0:T(8,128)(2,1)} %collective-permute-done.2.other_ref, ...), custom_call_target="tpu_custom_call" | custom-call | flops 6442450944 | bytes 22020096 | tf_op jit(solution)/shard_map/contract/pallas_call | solution.py:243
  (2 shorter events, 0.0 us)
Async XLA Ops:
  0.0 13.6 %collective-permute-start = (bf16[2,256,256]{2,1,0:T(8,128)(2,1)}, bf16[2,256,256]{2,1,0:T(8,128)(2,1)S(1)}, u32[]{:S(2)}, u32[]{:S(2)}) collective-permute-start(bf16[2,256,256]{2,1,0:T(8,128)(2,1)} %param.13), channel_id=1, source_target_pairs={{0,1},{1,0},{2,3},{3,2},{4,5},{5,4},{6,7},{7,6},{8,9},{9,8},{10,11... | collective-permute-start | bytes 786440 | tf_op jit(solution)/shard_map/ppermute | solution.py:271
  0.7 13.0 %collective-permute-start.1 = (s32[48,2]{0,1:T(2,128)}, s32[48,2]{0,1:T(2,128)S(1)}, u32[]{:S(2)}, u32[]{:S(2)}) collective-permute-start(s32[48,2]{0,1:T(2,128)} %param.10), channel_id=1, source_target_pairs={{0,1},{1,0},{2,3},{3,2},{4,5},{5,4},{6,7},{7,6},{8,9},{9,8},{10,11... | collective-permute-start | bytes 1160 | tf_op jit(solution)/shard_map/ppermute | solution.py:272
  269.0 4.8 %copy-start.1 = (s32[48,2]{0,1:T(2,128)S(1)}, s32[48,2]{0,1:T(2,128)}, u32[]{:S(2)}) copy-start(s32[48,2]{0,1:T(2,128)} %param.10) | copy-start | bytes 1156
  269.0 5.4 %copy-start = (bf16[2,256,256]{2,1,0:T(8,128)(2,1)S(1)}, bf16[2,256,256]{2,1,0:T(8,128)(2,1)}, u32[]{:S(2)}) copy-start(bf16[2,256,256]{2,1,0:T(8,128)(2,1)} %param.13) | copy-start | bytes 786436
  273.4 7.6 %collective-permute-start.2 = (bf16[128,64,256]{2,1,0:T(8,128)(2,1)}, bf16[128,64,256]{2,1,0:T(8,128)(2,1)}, u32[]{:S(2)}, u32[]{:S(2)}) collective-permute-start(bf16[128,64,256]{2,1,0:T(8,128)(2,1)} %get-tuple-element.21), channel_id=1, source_target_pairs={{0,1},{1,0},{2,3},{3,2},{4,5},{5,4},{6,7},{7,6},{8,9},{9,8},{10,11... | collective-permute-start | bytes 12582920 | tf_op jit(solution)/shard_map/ppermute | solution.py:284

commit v4 on v3

--- a/solution.py
+++ b/solution.py
@@ -8,7 +8,7 @@
 SWAP = [(0, 1), (1, 0)]
 TAIL = 8
 GROUP = 16
-STEP = 4
+STEP = 8
 LANES = 128
 HBM = pl.BlockSpec(memory_space=pltpu.HBM)
 
@@ -101,17 +101,47 @@
     )
 
 
-def split_kernel(got_ref, quarters_ref, places_ref, notes, quarter_sem, note_sem):
-    parcels, quarter, _ = quarters_ref.shape
+def split_kernel(got_ref, out_ref, staged, read_sems, write_sems):
+    parcels, quarter, _ = staged.shape
+    first = got_ref.shape[1] - TAIL - quarter
+    parts = read_sems.shape[0]
+    size = parcels // parts
+    reads, writes = [], []
+    for p in range(parts):
+        span = pl.ds(p * size, size)
+        reads.append(
+            copy(got_ref.at[span, pl.ds(first, quarter)], staged.at[span], read_sems.at[p])
+        )
+        writes.append(copy(staged.at[span], out_ref.at[span], write_sems.at[p]))
+        reads[p].start()
+    for p in range(parts):
+        reads[p].wait()
+        writes[p].start()
+    for p in range(parts):
+        writes[p].wait()
+
+
+def split(got, quarter):
+    parcels, rows, cols = got.shape
+    return pl.pallas_call(
+        split_kernel,
+        in_specs=[HBM],
+        out_specs=HBM,
+        scratch_shapes=[
+            pltpu.VMEM((parcels, quarter, cols), got.dtype),
+            pltpu.SemaphoreType.DMA((8,)),
+            pltpu.SemaphoreType.DMA((8,)),
+        ],
+        out_shape=jax.ShapeDtypeStruct((parcels, quarter, cols), got.dtype),
+        compiler_params=pltpu.CompilerParams(vmem_limit_bytes=60 << 20),
+        name="theta_quarters",
+    )(got)
+
+
+def places_kernel(got_ref, out_ref, notes, note_sem):
     end = got_ref.shape[1]
-    theta = copy(
-        got_ref.at[:, pl.ds(end - TAIL - quarter, quarter)], quarters_ref, quarter_sem
-    )
-    tails = copy(
-        got_ref.at[:, pl.ds(end - TAIL, TAIL), pl.ds(0, LANES)], notes, note_sem
-    )
+    tails = copy(got_ref.at[:, pl.ds(end - TAIL, TAIL), pl.ds(0, LANES)], notes, note_sem)
     tails.start()
-    theta.start()
     tails.wait()
     tail = notes[...].astype(jnp.float32)
     row = lax.broadcasted_iota(jnp.int32, tail.shape, 1)
@@ -122,42 +152,40 @@
     lands = (slot.astype(jnp.int32) == wanted) & (parcel % 2 == 0)
     anchor = jnp.sum(jnp.where(lands, parcel, 0), axis=0, keepdims=True)
     dims = jnp.sum(jnp.where(lands, live.astype(jnp.int32), 0), axis=0, keepdims=True)
-    places_ref[0:1, :] = anchor
-    places_ref[1:2, :] = dims
-    theta.wait()
-
-
-def split(got, quarter):
-    parcels, rows, cols = got.shape
+    out_ref[0:1, :] = anchor
+    out_ref[1:2, :] = dims
+
+
+def find_places(got):
+    parcels = got.shape[0]
     return pl.pallas_call(
-        split_kernel,
+        places_kernel,
         in_specs=[HBM],
-        out_specs=[pl.BlockSpec(memory_space=pltpu.VMEM)] * 2,
+        out_specs=pl.BlockSpec(memory_space=pltpu.VMEM),
         scratch_shapes=[
             pltpu.VMEM((parcels, TAIL, LANES), got.dtype),
             pltpu.SemaphoreType.DMA,
-            pltpu.SemaphoreType.DMA,
         ],
-        out_shape=[
-            jax.ShapeDtypeStruct((parcels, quarter, cols), got.dtype),
-            jax.ShapeDtypeStruct((2, LANES), jnp.int32),
-        ],
+        out_shape=jax.ShapeDtypeStruct((2, LANES), jnp.int32),
         compiler_params=pltpu.CompilerParams(vmem_limit_bytes=60 << 20),
-        name="split_parcels",
+        cost_estimate=pl.CostEstimate(flops=0, bytes_accessed=8 << 20, transcendentals=0),
+        name="places",
     )(got)
 
 
 def apply_kernel(
     places_ref, pairs_ref, core_ref, got_ref, other_ref, right_ref, out_ref,
-    theta, left, inner, rows_f32, theta_sems, left_sems,
+    theta, left, inner, even, odd, turned, theta_sems, left_sems, out_sems,
 ):
     slots, _, _, quarter, cols = theta.shape
     channels = left.shape[1] * left.shape[2]
     half, tile = 2 * quarter, 4 * quarter
     bulk = channels * half // 2
     core = core_ref[0]
-
-    def fetch_theta(j, carry):
+    groups, steps = slots // GROUP, GROUP // STEP
+    part = half // steps
+
+    def fetch(j, carry):
         source = places_ref[0, j]
         copy(
             got_ref.at[pl.ds(source, 2), pl.ds(bulk, quarter)],
@@ -167,22 +195,17 @@
         copy(other_ref.at[pl.ds(source, 2)], theta.at[j, 1 - core], theta_sems.at[j]).start()
         return carry
 
-    def fetch_left(j, carry):
-        source = places_ref[0, j]
+    lax.fori_loop(0, slots, fetch, 0)
+
+    strip = 16
+    strip_rows = lax.broadcasted_iota(jnp.int32, (strip, cols), 0)
+
+    def trim(j, carry):
         copy(
-            got_ref.at[pl.ds(source, 2), pl.ds(0, bulk)],
+            got_ref.at[pl.ds(places_ref[0, j], 2), pl.ds(0, bulk)],
             left.at[j].reshape(2, bulk, cols),
             left_sems.at[j],
         ).start()
-        return carry
-
-    lax.fori_loop(0, slots, fetch_theta, 0)
-    lax.fori_loop(0, slots, fetch_left, 0)
-
-    strip = 16
-    strip_rows = lax.broadcasted_iota(jnp.int32, (strip, cols), 0)
-
-    def trim(j, carry):
         copy(theta.at[j], theta.at[j], theta_sems.at[j]).wait()
         live = places_ref[1, j]
         block = theta.at[j].reshape(tile, cols)
@@ -200,12 +223,22 @@
 
     half_ids = lax.broadcasted_iota(jnp.int32, (half, cols), 0) + core * half
 
-    for g in range(slots // GROUP):
+    def turn(g, b):
+        first = pl.multiple_of(b * part, part)
+        rows = (even, odd)[g % 2][:, pl.ds(first, part), :]
+        turned[g, pl.ds(first, part)] = pltpu.einshape("krn->rkn", rows).astype(turned.dtype)
+
+    def write(g):
+        return copy(turned.at[g], out_ref.at[:, pl.ds(g * GROUP, GROUP)], out_sems.at[g])
+
+    for g in range(groups):
 
         def contract(b, carry):
             for k in range(STEP):
                 j = g * GROUP + b * STEP + k
                 copy(left.at[j], left.at[j], left_sems.at[j]).wait()
+            for k in range(STEP):
+                j = g * GROUP + b * STEP + k
                 for w in range(channels):
                     partner = theta[pairs_ref[w, j]].reshape(tile, cols)
                     inner[k * half:(k + 1) * half, w * cols:(w + 1) * cols] = jnp.dot(
@@ -213,25 +246,27 @@
                         partner,
                         preferred_element_type=jnp.float32,
                     ).astype(inner.dtype)
+            if g > 0:
+                turn(g - 1, b)
             total = jnp.dot(
                 inner[...], right_ref[...], preferred_element_type=jnp.float32
             )
             for k in range(STEP):
-                j = g * GROUP + b * STEP + k
-                kept = jnp.where(
-                    half_ids < places_ref[1, j], total[k * half:(k + 1) * half], 0.0
+                live = places_ref[1, g * GROUP + b * STEP + k]
+                (even, odd)[g % 2][b * STEP + k] = jnp.where(
+                    half_ids < live, total[k * half:(k + 1) * half], 0.0
                 )
-                for side in range(2):
-                    rows_f32[side, pl.ds(b * STEP + k, half, stride=GROUP)] = kept[
-                        :, side * LANES:(side + 1) * LANES
-                    ]
             return carry
 
-        lax.fori_loop(0, GROUP // STEP, contract, 0)
-        for side in range(2):
-            out_ref[:, g * GROUP:(g + 1) * GROUP, side * LANES:(side + 1) * LANES] = (
-                rows_f32[side].reshape(half, GROUP, LANES).astype(out_ref.dtype)
-            )
+        lax.fori_loop(0, steps, contract, 0)
+        if g > 0:
+            write(g - 1).start()
+
+    for b in range(steps):
+        turn(groups - 1, b)
+    write(groups - 1).start()
+    for g in range(groups):
+        write(g).wait()
 
 
 def apply(places, pairs, core, got, other, right, dtype):
@@ -246,14 +281,17 @@
             num_scalar_prefetch=3,
             grid=(),
             in_specs=[HBM, HBM, pl.BlockSpec(memory_space=pltpu.VMEM)],
-            out_specs=pl.BlockSpec(memory_space=pltpu.VMEM),
+            out_specs=HBM,
             scratch_shapes=[
                 pltpu.VMEM((slots, 2, 2, quarter, cols), dtype),
                 pltpu.VMEM((slots, 2, channels // 2, half, cols), dtype),
                 pltpu.VMEM((STEP * half, channels * cols), dtype),
-                pltpu.VMEM((2, half * GROUP, LANES), jnp.float32),
+                pltpu.VMEM((GROUP, half, cols), jnp.float32),
+                pltpu.VMEM((GROUP, half, cols), jnp.float32),
+                pltpu.VMEM((slots // GROUP, half, GROUP, cols), dtype),
                 pltpu.SemaphoreType.DMA((slots,)),
                 pltpu.SemaphoreType.DMA((slots,)),
+                pltpu.SemaphoreType.DMA((slots // GROUP,)),
             ],
         ),
         out_shape=jax.ShapeDtypeStruct((half, slots, cols), dtype),
@@ -280,8 +318,8 @@
     got, right_other, pairs_other, core = lax.optimization_barrier(
         (got, right_other, pairs_other, core)
     )
-    quarters, places = split(got, theta_blocks.shape[1] // 4)
-    other = lax.ppermute(quarters, "mpo", SWAP)
+    other = lax.ppermute(split(got, theta_blocks.shape[1] // 4), "mpo", SWAP)
+    places = find_places(got)
     first = core == 0
     pairs = jnp.concatenate(
         [jnp.where(first, block_pairs, pairs_other), jnp.where(first, pairs_other, block_pairs)],

time: 305 us -> 296 us (0.970)
  Pallas kernels: 41.4 us -> 34.2 us
    pallas_call x1, Pallas kernels: 24.1 us -> 15.7 us  [apply(): pl.pallas_call(apply_kernel, grid_spec=pltpu.PrefetchScalarGridSpec(num_s...]
  transfers between devices with their start and end apart: 3 -> 3, of which waited for: 1 -> 1; matrix products, arithmetic and copies ran while one was open for 0% -> 1% of each run, Pallas kernels for 4% -> 5%
where the time goes in v4:
time: 296 us
  blocking collectives  255 us (86%)
  Pallas kernels  34.2 us (12%)
  waiting for transfers between devices  3.64 us (1%)
    all_to_all x1, blocking collectives, on_device(): lax.all_to_all(parcels, ('sec', 'mpo'), split_axis=0, concat_axis=0, tile...  255 us
    pallas_call x1, Pallas kernels, apply(): pl.pallas_call(apply_kernel, grid_spec=pltpu.PrefetchScalarGridSpec(num_s...  15.7 us
    pallas_call x1, Pallas kernels, pack(): pl.pallas_call(pack_kernel, grid_spec=pltpu.PrefetchScalarGridSpec(num_sc...  12.9 us
  transfers between devices with their start and end apart: 3, of which 1 were waited for; matrix products, arithmetic and copies ran while one was open for 1% of the time, Pallas kernels for 5%

profile of v4, /device:TPU:11, one launch (start us, length us, event | category | flops | bytes accessed | tf_op | source)
XLA Modules:
  0.0 296.0 jit_solution(2540440612183395016)
XLA Ops:
  0.0 0.7 collective-permute-start
  0.7 0.0 collective-permute-start.1
  0.7 12.9 %pack_parcels.1 = bf16[128,328,256]{2,1,0:T(8,128)(2,1)} custom-call(s32[48]{0:T(128)} %owner_ref.1, s32[48]{0:T(128)} %slot_ref.1, s32[48]{0:T(128)} %dims_ref.1, s32[1]{0:T(128)} %bitcast.core_ref, bf16[48,2,2,64,256]{4,3,2,1,0:T(8,128)(2,1)} %bitcast.7, bf16[48,2,2,128,256]{4,3,2,1,0:T(8,128)(2,1)} %bitcast.6), custom_call_target="tpu_custom_call" | custom-call | bytes 32243712 | tf_op jit(solution)/shard_map/pack_parcels/pallas_call | solution.py:78
  13.6 0.0 collective-permute-done.1
  13.6 0.0 collective-permute-done
  13.7 255.4 %all_to_all.5.got_ref = bf16[128,328,256]{2,1,0:T(8,128)(2,1)} all-to-all(bf16[128,328,256]{2,1,0:T(8,128)(2,1)} %pack_parcels.1), channel_id=1, replica_groups=mesh['sec'=64,'mpo'=2] {'sec','mpo'}, dimensions={0} | all-to-all | bytes 42991616 | tf_op jit(solution)/shard_map/all_to_all | solution.py:317
  269.0 3.6 %theta_quarters.1 = bf16[128,64,256]{2,1,0:T(8,128)(2,1)} custom-call(bf16[128,328,256]{2,1,0:T(8,128)(2,1)} %all_to_all.5.got_ref), custom_call_target="tpu_custom_call" | custom-call | tf_op jit(solution)/shard_map/theta_quarters/pallas_call | solution.py:126
  272.7 0.0 copy-start.1
  272.7 0.0 copy-start
  272.7 0.5 collective-permute-start.2
  273.2 2.0 places.1.places_ref
  275.2 0.0 copy-done.1
  275.2 0.6 add_bitcast_fusion.pairs_ref
  275.8 0.0 copy-done
  275.8 0.9 pad_maximum_fusion
  276.7 3.6 %collective-permute-done.2.other_ref = bf16[128,64,256]{2,1,0:T(8,128)(2,1)} collective-permute-done((bf16[128,64,256]{2,1,0:T(8,128)(2,1)}, bf16[128,64,256]{2,1,0:T(8,128)(2,1)}, u32[]{:S(2)}, u32[]{:S(2)}) %collective-permute-start.2) | collective-permute-done | bytes 4194336 | tf_op jit(solution)/shard_map/ppermute | solution.py:321
  280.3 15.7 %contract.1 = bf16[128,48,256]{2,1,0:T(8,128)(2,1)} custom-call(s32[2,128]{1,0:T(2,128)} %places.1.places_ref, s32[4,48]{1,0:T(4,128)} %add_bitcast_fusion.pairs_ref, s32[1]{0:T(128)} %bitcast.core_ref, bf16[128,328,256]{2,1,0:T(8,128)(2,1)} %all_to_all.5.got_ref, bf16[128,64,256]{2,1,0:T(8,128)(2,1)} %collective-permute-done.2.other_ref, ...), custom_call_target="tpu_custom_call" | custom-call | flops 6442450944 | bytes 22020096 | tf_op jit(solution)/shard_map/contract/pallas_call | solution.py:278
  (2 shorter events, 0.0 us)
Async XLA Ops:
  0.0 13.6 %collective-permute-start = (bf16[2,256,256]{2,1,0:T(8,128)(2,1)}, bf16[2,256,256]{2,1,0:T(8,128)(2,1)S(1)}, u32[]{:S(2)}, u32[]{:S(2)}) collective-permute-start(bf16[2,256,256]{2,1,0:T(8,128)(2,1)} %param.13), channel_id=1, source_target_pairs={{0,1},{1,0},{2,3},{3,2},{4,5},{5,4},{6,7},{7,6},{8,9},{9,8},{10,11... | collective-permute-start | bytes 786440 | tf_op jit(solution)/shard_map/ppermute | solution.py:309
  0.7 13.0 %collective-permute-start.1 = (s32[48,2]{0,1:T(2,128)}, s32[48,2]{0,1:T(2,128)S(1)}, u32[]{:S(2)}, u32[]{:S(2)}) collective-permute-start(s32[48,2]{0,1:T(2,128)} %param.10), channel_id=1, source_target_pairs={{0,1},{1,0},{2,3},{3,2},{4,5},{5,4},{6,7},{7,6},{8,9},{9,8},{10,11... | collective-permute-start | bytes 1160 | tf_op jit(solution)/shard_map/ppermute | solution.py:310
  272.7 2.5 copy-start.1
  272.7 3.1 %copy-start = (bf16[2,256,256]{2,1,0:T(8,128)(2,1)S(1)}, bf16[2,256,256]{2,1,0:T(8,128)(2,1)}, u32[]{:S(2)}) copy-start(bf16[2,256,256]{2,1,0:T(8,128)(2,1)} %param.13) | copy-start | bytes 786436
  272.7 7.6 %collective-permute-start.2 = (bf16[128,64,256]{2,1,0:T(8,128)(2,1)}, bf16[128,64,256]{2,1,0:T(8,128)(2,1)}, u32[]{:S(2)}, u32[]{:S(2)}) collective-permute-start(bf16[128,64,256]{2,1,0:T(8,128)(2,1)} %theta_quarters.1), channel_id=1, source_target_pairs={{0,1},{1,0},{2,3},{3,2},{4,5},{5,4},{6,7},{7,6},{8,9},{9,8},{10,11... | collective-permute-start | bytes 12582920 | tf_op jit(solution)/shard_map/ppermute | solution.py:321

commit v5 on v4

--- a/solution.py
+++ b/solution.py
@@ -1,3 +1,5 @@
+import functools
+
 import jax
 import jax.numpy as jnp
 from jax import lax
@@ -19,51 +21,59 @@
 
 def pack_kernel(
     owner_ref, slot_ref, dims_ref, core_ref, theta_ref, left_ref, out_ref,
-    staged, blank, load_sems, store_sems, blank_sem,
+    left, theta, notes, blank, load_sems, store_sems, blank_sem,
 ):
     slots, channels, _, half, cols = left_ref.shape
     quarter = half // 2
     bulk = channels * half
+    sides = cols // LANES
+    body = sides * (bulk + quarter)
     core = core_ref[0]
 
     def load(i, carry):
-        for h in range(2):
-            copy(
-                left_ref.at[i, :, h],
-                staged.at[i, h, pl.ds(0, bulk)].reshape(channels, half, cols),
-                load_sems.at[i],
-            ).start()
-        copy(
-            theta_ref.at[i, :, core],
-            staged.at[i, :, pl.ds(bulk, quarter)],
-            load_sems.at[i],
-        ).start()
+        copy(left_ref.at[i], left.at[i], load_sems.at[0, i]).start()
+        copy(theta_ref.at[i, :, core], theta.at[i], load_sems.at[1, i]).start()
         return carry
 
     lax.fori_loop(0, slots, load, 0)
 
     blank[...] = jnp.zeros_like(blank)
-    clear = copy(blank, out_ref.at[:, pl.ds(bulk + quarter, TAIL)], blank_sem)
+    clear = copy(blank, out_ref.at[:, pl.ds(body, TAIL)], blank_sem)
     clear.start()
     clear.wait()
-    tail_rows = lax.broadcasted_iota(jnp.int32, (TAIL, cols), 0)
+    tail_rows = lax.broadcasted_iota(jnp.int32, (2, TAIL, LANES), 1)
 
     def store(i, carry):
-        note = jnp.where(tail_rows == 0, slot_ref[i] + 1, dims_ref[i])
-        note = note.astype(jnp.float32).astype(staged.dtype)
-        for h in range(2):
-            staged[i, h, bulk + quarter:] = note
-        body = staged.at[i, :, pl.ds(0, bulk + quarter)]
-        copy(body, body, load_sems.at[i]).wait()
+        text = jnp.where(tail_rows == 0, slot_ref[i] + 1, dims_ref[i])
+        notes[i] = text.astype(jnp.float32).astype(notes.dtype)
         place = 2 * owner_ref[i]
-        copy(staged.at[i], out_ref.at[pl.ds(place, 2)], store_sems.at[i]).start()
+        pair = pl.ds(place, 2)
+        copy(notes.at[i], out_ref.at[pair, pl.ds(body, TAIL)], store_sems.at[i]).start()
+        copy(left_ref.at[i], left.at[i], load_sems.at[0, i]).wait()
+        for c in range(sides):
+            lanes = pl.ds(c * LANES, LANES)
+            for h in range(2):
+                copy(
+                    left.at[i, :, h, :, lanes],
+                    out_ref.at[place + h, pl.ds(c * bulk, bulk)].reshape(
+                        channels, half, LANES
+                    ),
+                    store_sems.at[i],
+                ).start()
+        copy(theta_ref.at[i, :, core], theta.at[i], load_sems.at[1, i]).wait()
+        for c in range(sides):
+            copy(
+                theta.at[i, :, :, pl.ds(c * LANES, LANES)],
+                out_ref.at[pair, pl.ds(sides * bulk + c * quarter, quarter)],
+                store_sems.at[i],
+            ).start()
         return carry
 
     lax.fori_loop(0, slots, store, 0)
 
     def settle(i, carry):
-        place = 2 * owner_ref[i]
-        copy(staged.at[i], out_ref.at[pl.ds(place, 2)], store_sems.at[i]).wait()
+        pair = out_ref.at[pl.ds(2 * owner_ref[i], 2)]
+        copy(pair, pair, store_sems.at[i]).wait()
         return carry
 
     lax.fori_loop(0, slots, settle, 0)
@@ -72,9 +82,9 @@
 def pack(new_owner, new_slot, sector_dims, core, theta_blocks, left_env, peers):
     slots, channels, tile, cols = left_env.shape
     half, quarter = tile // 2, tile // 4
-    rows = channels * half + quarter + TAIL
+    rows = (cols // LANES) * (channels * half + quarter) + TAIL
     dtype = theta_blocks.dtype
-    moved = 2 * slots * 2 * rows * cols * 2
+    moved = 2 * slots * 2 * rows * LANES * 2
     return pl.pallas_call(
         pack_kernel,
         grid_spec=pltpu.PrefetchScalarGridSpec(
@@ -83,14 +93,16 @@
             in_specs=[HBM] * 2,
             out_specs=HBM,
             scratch_shapes=[
-                pltpu.VMEM((slots, 2, rows, cols), dtype),
-                pltpu.VMEM((2 * peers, TAIL, cols), dtype),
-                pltpu.SemaphoreType.DMA((slots,)),
+                pltpu.VMEM((slots, channels, 2, half, cols), dtype),
+                pltpu.VMEM((slots, 2, quarter, cols), dtype),
+                pltpu.VMEM((slots, 2, TAIL, LANES), dtype),
+                pltpu.VMEM((2 * peers, TAIL, LANES), dtype),
+                pltpu.SemaphoreType.DMA((2, slots)),
                 pltpu.SemaphoreType.DMA((slots,)),
                 pltpu.SemaphoreType.DMA,
             ],
         ),
-        out_shape=jax.ShapeDtypeStruct((2 * peers, rows, cols), dtype),
+        out_shape=jax.ShapeDtypeStruct((2 * peers, rows, LANES), dtype),
         compiler_params=pltpu.CompilerParams(vmem_limit_bytes=60 << 20),
         cost_estimate=pl.CostEstimate(flops=0, bytes_accessed=moved, transcendentals=0),
         name="pack_parcels",
@@ -101,9 +113,8 @@
     )
 
 
-def split_kernel(got_ref, out_ref, staged, read_sems, write_sems):
+def split_kernel(first, got_ref, out_ref, staged, read_sems, write_sems):
     parcels, quarter, _ = staged.shape
-    first = got_ref.shape[1] - TAIL - quarter
     parts = read_sems.shape[0]
     size = parcels // parts
     reads, writes = [], []
@@ -121,26 +132,26 @@
         writes[p].wait()
 
 
-def split(got, quarter):
-    parcels, rows, cols = got.shape
+def split(got, first, quarter):
+    parcels = got.shape[0]
     return pl.pallas_call(
-        split_kernel,
+        functools.partial(split_kernel, first),
         in_specs=[HBM],
         out_specs=HBM,
         scratch_shapes=[
-            pltpu.VMEM((parcels, quarter, cols), got.dtype),
-            pltpu.SemaphoreType.DMA((8,)),
-            pltpu.SemaphoreType.DMA((8,)),
+            pltpu.VMEM((parcels, quarter, LANES), got.dtype),
+            pltpu.SemaphoreType.DMA((4,)),
+            pltpu.SemaphoreType.DMA((4,)),
         ],
-        out_shape=jax.ShapeDtypeStruct((parcels, quarter, cols), got.dtype),
+        out_shape=jax.ShapeDtypeStruct((parcels, quarter, LANES), got.dtype),
         compiler_params=pltpu.CompilerParams(vmem_limit_bytes=60 << 20),
+        cost_estimate=pl.CostEstimate(flops=0, bytes_accessed=8 << 20, transcendentals=0),
         name="theta_quarters",
     )(got)
 
 
 def places_kernel(got_ref, out_ref, notes, note_sem):
-    end = got_ref.shape[1]
-    tails = copy(got_ref.at[:, pl.ds(end - TAIL, TAIL), pl.ds(0, LANES)], notes, note_sem)
+    tails = copy(got_ref.at[:, pl.ds(got_ref.shape[1] - TAIL, TAIL)], notes, note_sem)
     tails.start()
     tails.wait()
     tail = notes[...].astype(jnp.float32)
@@ -173,26 +184,28 @@
     )(got)
 
 
-def apply_kernel(
-    places_ref, pairs_ref, core_ref, got_ref, other_ref, right_ref, out_ref,
-    theta, left, inner, even, odd, turned, theta_sems, left_sems, out_sems,
-):
+def apply_kernel(sides, places_ref, pairs_ref, core_ref, got_ref, *refs):
+    others_ref, right_ref, out_ref = refs[:sides], refs[sides], refs[sides + 1]
+    theta, left, inner, even, odd, turned, theta_sems, left_sems, out_sems = refs[sides + 2:]
     slots, _, _, quarter, cols = theta.shape
-    channels = left.shape[1] * left.shape[2]
-    half, tile = 2 * quarter, 4 * quarter
-    bulk = channels * half // 2
+    half, tile, bulk = 2 * quarter, 4 * quarter, left.shape[2]
+    channels = 2 * bulk // half
     core = core_ref[0]
     groups, steps = slots // GROUP, GROUP // STEP
     part = half // steps
 
     def fetch(j, carry):
-        source = places_ref[0, j]
-        copy(
-            got_ref.at[pl.ds(source, 2), pl.ds(bulk, quarter)],
-            theta.at[j, core],
-            theta_sems.at[j],
-        ).start()
-        copy(other_ref.at[pl.ds(source, 2)], theta.at[j, 1 - core], theta_sems.at[j]).start()
+        pair = pl.ds(places_ref[0, j], 2)
+        for c in range(sides):
+            lanes = pl.ds(c * LANES, LANES)
+            copy(
+                got_ref.at[pair, pl.ds(sides * bulk + c * quarter, quarter)],
+                theta.at[j, core, :, :, lanes],
+                theta_sems.at[j],
+            ).start()
+            copy(
+                others_ref[c].at[pair], theta.at[j, 1 - core, :, :, lanes], theta_sems.at[j]
+            ).start()
         return carry
 
     lax.fori_loop(0, slots, fetch, 0)
@@ -201,13 +214,15 @@
     strip_rows = lax.broadcasted_iota(jnp.int32, (strip, cols), 0)
 
     def trim(j, carry):
-        copy(
-            got_ref.at[pl.ds(places_ref[0, j], 2), pl.ds(0, bulk)],
-            left.at[j].reshape(2, bulk, cols),
-            left_sems.at[j],
-        ).start()
+        for c in range(sides):
+            copy(
+                got_ref.at[pl.ds(places_ref[0, j], 2), pl.ds(c * bulk, bulk)],
+                left.at[j, :, :, pl.ds(c * LANES, LANES)],
+                left_sems.at[j],
+            ).start()
         copy(theta.at[j], theta.at[j], theta_sems.at[j]).wait()
         live = places_ref[1, j]
+
         block = theta.at[j].reshape(tile, cols)
 
         def clear(t, inner_carry):
@@ -240,10 +255,9 @@
             for k in range(STEP):
                 j = g * GROUP + b * STEP + k
                 for w in range(channels):
-                    partner = theta[pairs_ref[w, j]].reshape(tile, cols)
                     inner[k * half:(k + 1) * half, w * cols:(w + 1) * cols] = jnp.dot(
-                        left[j, w // 2, w % 2],
-                        partner,
+                        left[j, w // 2, pl.ds(w % 2 * half, half)],
+                        theta[pairs_ref[w, j]].reshape(tile, cols),
                         preferred_element_type=jnp.float32,
                     ).astype(inner.dtype)
             if g > 0:
@@ -269,22 +283,22 @@
         write(g).wait()
 
 
-def apply(places, pairs, core, got, other, right, dtype):
+def apply(places, pairs, core, got, others, right, dtype):
     channels, tile, cols = right.shape
     slots = pairs.shape[1]
     half, quarter = tile // 2, tile // 4
     flops = 4 * slots * channels * half * tile * cols
     moved = 2 * slots * cols * (tile + channels * half + half)
     return pl.pallas_call(
-        apply_kernel,
+        functools.partial(apply_kernel, cols // LANES),
         grid_spec=pltpu.PrefetchScalarGridSpec(
             num_scalar_prefetch=3,
             grid=(),
-            in_specs=[HBM, HBM, pl.BlockSpec(memory_space=pltpu.VMEM)],
+            in_specs=[HBM] * (1 + len(others)) + [pl.BlockSpec(memory_space=pltpu.VMEM)],
             out_specs=HBM,
             scratch_shapes=[
                 pltpu.VMEM((slots, 2, 2, quarter, cols), dtype),
-                pltpu.VMEM((slots, 2, channels // 2, half, cols), dtype),
+                pltpu.VMEM((slots, 2, channels * half // 2, cols), dtype),
                 pltpu.VMEM((STEP * half, channels * cols), dtype),
                 pltpu.VMEM((GROUP, half, cols), jnp.float32),
                 pltpu.VMEM((GROUP, half, cols), jnp.float32),
@@ -298,7 +312,7 @@
         compiler_params=pltpu.CompilerParams(vmem_limit_bytes=60 << 20),
         cost_estimate=pl.CostEstimate(flops=flops, bytes_accessed=moved, transcendentals=0),
         name="contract",
-    )(places, pairs, core, got, other, right.reshape(channels * tile, cols))
+    )(places, pairs, core, got, *others, right.reshape(channels * tile, cols))
 
 
 def on_device(sector_dims, new_owner, new_slot, block_pairs, theta_blocks, left_env, right_env):
@@ -318,7 +332,12 @@
     got, right_other, pairs_other, core = lax.optimization_barrier(
         (got, right_other, pairs_other, core)
     )
-    other = lax.ppermute(split(got, theta_blocks.shape[1] // 4), "mpo", SWAP)
+    channels, tile, cols = left_env.shape[1:]
+    bulk = (cols // LANES) * channels * tile // 2
+    others = [
+        lax.ppermute(split(got, bulk + c * tile // 4, tile // 4), "mpo", SWAP)
+        for c in range(cols // LANES)
+    ]
     places = find_places(got)
     first = core == 0
     pairs = jnp.concatenate(
@@ -329,7 +348,7 @@
         [jnp.where(first, right_env, right_other), jnp.where(first, right_other, right_env)],
         axis=0,
     )
-    return apply(places, pairs, core_word, got, other, right, theta_blocks.dtype)
+    return apply(places, pairs, core_word, got, others, right, theta_blocks.dtype)
 
 
 def solution(mesh):

time: 296 us -> 295 us (level)
    pallas_call x2 -> x3, Pallas kernels: 19.3 us -> 20.6 us  [the longest x1 15.7 us: apply(): pl.pallas_call(functools.partial(apply_kernel, cols // LANES), grid_spec=...]
  transfers between devices with their start and end apart: 3 -> 4, of which waited for: 1 -> 2; matrix products, arithmetic and copies ran while one was open for 1% -> 1% of each run, Pallas kernels for 5% -> 5%
where the time goes in v5:
time: 295 us
  blocking collectives  253 us (86%)
  Pallas kernels  35.6 us (12%)
  waiting for transfers between devices  3.47 us (1%)
    all_to_all x1, blocking collectives, on_device(): lax.all_to_all(parcels, ('sec', 'mpo'), split_axis=0, concat_axis=0, tile...  253 us
    pallas_call x1, Pallas kernels, apply(): pl.pallas_call(functools.partial(apply_kernel, cols // LANES), grid_spec=...  15.7 us
    pallas_call x1, Pallas kernels, pack(): pl.pallas_call(pack_kernel, grid_spec=pltpu.PrefetchScalarGridSpec(num_sc...  13 us
  transfers between devices with their start and end apart: 4, of which 2 were waited for; matrix products, arithmetic and copies ran while one was open for 1% of the time, Pallas kernels for 5%

profile of v5, /device:TPU:11, one launch (start us, length us, event | category | flops | bytes accessed | tf_op | source)
XLA Modules:
  0.0 294.8 jit_solution(5136949861491417345)
XLA Ops:
  0.0 0.7 collective-permute-start
  0.7 0.0 collective-permute-start.1
  0.7 13.0 %pack_parcels.1 = bf16[128,648,128]{2,1,0:T(8,128)(2,1)} custom-call(s32[48]{0:T(128)} %owner_ref.1, s32[48]{0:T(128)} %slot_ref.1, s32[48]{0:T(128)} %dims_ref.1, s32[1]{0:T(128)} %bitcast.core_ref, bf16[48,2,2,64,256]{4,3,2,1,0:T(8,128)(2,1)} %bitcast.7, bf16[48,2,2,128,256]{4,3,2,1,0:T(8,128)(2,1)} %bitcast.6), custom_call_target="tpu_custom_call" | custom-call | bytes 31850496 | tf_op jit(solution)/shard_map/pack_parcels/pallas_call | solution.py:88
  13.7 0.0 collective-permute-done.1
  13.7 0.0 collective-permute-done
  13.7 252.8 %all_to_all.5.got_ref = bf16[128,648,128]{2,1,0:T(8,128)(2,1)} all-to-all(bf16[128,648,128]{2,1,0:T(8,128)(2,1)} %pack_parcels.1), channel_id=1, replica_groups=mesh['sec'=64,'mpo'=2] {'sec','mpo'}, dimensions={0} | all-to-all | bytes 42467328 | tf_op jit(solution)/shard_map/all_to_all | solution.py:331
  266.5 2.5 theta_quarters.3
  269.0 2.4 theta_quarters.2
  271.4 0.0 copy-start.2
  271.4 0.0 copy-start.1
  271.5 0.5 collective-permute-start.2
  271.9 0.1 collective-permute-start.3
  272.0 2.0 places.1.places_ref
  274.1 0.0 copy-done.2
  274.1 0.6 add_bitcast_fusion.pairs_ref
  274.7 0.0 copy-done.1
  274.7 0.9 pad_maximum_fusion
  275.6 2.2 collective-permute-done.2.refs_0_
  277.8 0.0 copy-start
  277.8 1.3 collective-permute-done.3.refs_1_
  279.1 0.0 copy-done
  279.1 15.7 %contract.1 = bf16[128,48,256]{2,1,0:T(8,128)(2,1)} custom-call(s32[2,128]{1,0:T(2,128)} %places.1.places_ref, s32[4,48]{1,0:T(4,128)} %add_bitcast_fusion.pairs_ref, s32[1]{0:T(128)} %bitcast.core_ref, bf16[128,648,128]{2,1,0:T(8,128)(2,1)} %all_to_all.5.got_ref, bf16[128,64,128]{2,1,0:T(8,128)(2,1)} %copy-done, ...), custom_call_target="tpu_custom_call" | custom-call | flops 6442450944 | bytes 22020096 | tf_op jit(solution)/shard_map/contract/pallas_call | solution.py:292
  (2 shorter events, 0.0 us)
Async XLA Ops:
  0.0 13.7 %collective-permute-start = (bf16[2,256,256]{2,1,0:T(8,128)(2,1)}, bf16[2,256,256]{2,1,0:T(8,128)(2,1)S(1)}, u32[]{:S(2)}, u32[]{:S(2)}) collective-permute-start(bf16[2,256,256]{2,1,0:T(8,128)(2,1)} %param.13), channel_id=1, source_target_pairs={{0,1},{1,0},{2,3},{3,2},{4,5},{5,4},{6,7},{7,6},{8,9},{9,8},{10,11... | collective-permute-start | bytes 786440 | tf_op jit(solution)/shard_map/ppermute | solution.py:323
  0.7 13.0 %collective-permute-start.1 = (s32[48,2]{0,1:T(2,128)}, s32[48,2]{0,1:T(2,128)S(1)}, u32[]{:S(2)}, u32[]{:S(2)}) collective-permute-start(s32[48,2]{0,1:T(2,128)} %param.10), channel_id=1, source_target_pairs={{0,1},{1,0},{2,3},{3,2},{4,5},{5,4},{6,7},{7,6},{8,9},{9,8},{10,11... | collective-permute-start | bytes 1160 | tf_op jit(solution)/shard_map/ppermute | solution.py:324
  271.4 2.6 copy-start.2
  271.4 3.2 %copy-start.1 = (bf16[2,256,256]{2,1,0:T(8,128)(2,1)S(1)}, bf16[2,256,256]{2,1,0:T(8,128)(2,1)}, u32[]{:S(2)}) copy-start(bf16[2,256,256]{2,1,0:T(8,128)(2,1)} %param.13) | copy-start | bytes 786436
  271.5 6.3 %collective-permute-start.2 = (bf16[128,64,128]{2,1,0:T(8,128)(2,1)}, bf16[128,64,128]{2,1,0:T(8,128)(2,1)S(1)}, u32[]{:S(2)}, u32[]{:S(2)}) collective-permute-start(bf16[128,64,128]{2,1,0:T(8,128)(2,1)} %theta_quarters.2), channel_id=1, source_target_pairs={{0,1},{1,0},{2,3},{3,2},{4,5},{5,4},{6,7},{7,6},{8,9},{9,8},{10,11... | collective-permute-start | bytes 6291464 | tf_op jit(solution)/shard_map/ppermute | solution.py:338
  271.9 7.1 %collective-permute-start.3 = (bf16[128,64,128]{2,1,0:T(8,128)(2,1)}, bf16[128,64,128]{2,1,0:T(8,128)(2,1)}, u32[]{:S(2)}, u32[]{:S(2)}) collective-permute-start(bf16[128,64,128]{2,1,0:T(8,128)(2,1)} %theta_quarters.3), channel_id=1, source_target_pairs={{0,1},{1,0},{2,3},{3,2},{4,5},{5,4},{6,7},{7,6},{8,9},{9,8},{10,11... | collective-permute-start | bytes 6291464 | tf_op jit(solution)/shard_map/ppermute | solution.py:338
  277.8 1.3 copy-start

commit v6 on v5

--- a/solution.py
+++ b/solution.py
@@ -113,38 +113,29 @@
     )
 
 
-def split_kernel(first, got_ref, out_ref, staged, read_sems, write_sems):
-    parcels, quarter, _ = staged.shape
-    parts = read_sems.shape[0]
-    size = parcels // parts
-    reads, writes = [], []
-    for p in range(parts):
-        span = pl.ds(p * size, size)
-        reads.append(
-            copy(got_ref.at[span, pl.ds(first, quarter)], staged.at[span], read_sems.at[p])
-        )
-        writes.append(copy(staged.at[span], out_ref.at[span], write_sems.at[p]))
-        reads[p].start()
-    for p in range(parts):
-        reads[p].wait()
-        writes[p].start()
-    for p in range(parts):
-        writes[p].wait()
-
-
-def split(got, first, quarter):
+def split_kernel(first, got_ref, *refs):
+    outs_ref, sems = refs[:-1], refs[-1]
+    quarter = outs_ref[0].shape[1]
+    moves = [
+        copy(got_ref.at[:, pl.ds(first + c * quarter, quarter)], out_ref, sems.at[c])
+        for c, out_ref in enumerate(outs_ref)
+    ]
+    for move in moves:
+        move.start()
+    for move in moves:
+        move.wait()
+
+
+def split(got, first, quarter, sides):
     parcels = got.shape[0]
+    part = jax.ShapeDtypeStruct((parcels, quarter, LANES), got.dtype)
     return pl.pallas_call(
         functools.partial(split_kernel, first),
         in_specs=[HBM],
-        out_specs=HBM,
-        scratch_shapes=[
-            pltpu.VMEM((parcels, quarter, LANES), got.dtype),
-            pltpu.SemaphoreType.DMA((4,)),
-            pltpu.SemaphoreType.DMA((4,)),
-        ],
-        out_shape=jax.ShapeDtypeStruct((parcels, quarter, LANES), got.dtype),
-        compiler_params=pltpu.CompilerParams(vmem_limit_bytes=60 << 20),
+        out_specs=[pl.BlockSpec(memory_space=pltpu.VMEM)] * sides,
+        scratch_shapes=[pltpu.SemaphoreType.DMA((sides,))],
+        out_shape=[part] * sides,
+        compiler_params=pltpu.CompilerParams(vmem_limit_bytes=44 << 20),
         cost_estimate=pl.CostEstimate(flops=0, bytes_accessed=8 << 20, transcendentals=0),
         name="theta_quarters",
     )(got)
@@ -335,8 +326,8 @@
     channels, tile, cols = left_env.shape[1:]
     bulk = (cols // LANES) * channels * tile // 2
     others = [
-        lax.ppermute(split(got, bulk + c * tile // 4, tile // 4), "mpo", SWAP)
-        for c in range(cols // LANES)
+        lax.ppermute(quarters, "mpo", SWAP)
+        for quarters in split(got, bulk, tile // 4, cols // LANES)
     ]
     places = find_places(got)
     first = core == 0

time: 295 us -> 293 us (level)
  no operation moved by 1% of the time
where the time goes in v6:
time: 293 us
  blocking collectives  253 us (86%)
  Pallas kernels  34.3 us (12%)
  waiting for transfers between devices  3.19 us (1%)
    all_to_all x1, blocking collectives, on_device(): lax.all_to_all(parcels, ('sec', 'mpo'), split_axis=0, concat_axis=0, tile...  253 us
    pallas_call x1, Pallas kernels, apply(): pl.pallas_call(functools.partial(apply_kernel, cols // LANES), grid_spec=...  15.7 us
    pallas_call x1, Pallas kernels, pack(): pl.pallas_call(pack_kernel, grid_spec=pltpu.PrefetchScalarGridSpec(num_sc...  13 us
  transfers between devices with their start and end apart: 4, of which 2 were waited for; matrix products, arithmetic and copies ran while one was open for 1% of the time, Pallas kernels for 5%

profile of v6, /device:TPU:11, one launch (start us, length us, event | category | flops | bytes accessed | tf_op | source)
XLA Modules:
  0.0 293.1 jit_solution(15026278363838359228)
XLA Ops:
  0.0 0.7 collective-permute-start
  0.7 0.0 collective-permute-start.1
  0.7 13.0 %pack_parcels.1 = bf16[128,648,128]{2,1,0:T(8,128)(2,1)} custom-call(s32[48]{0:T(128)} %owner_ref.1, s32[48]{0:T(128)} %slot_ref.1, s32[48]{0:T(128)} %dims_ref.1, s32[1]{0:T(128)} %bitcast.core_ref, bf16[48,2,2,64,256]{4,3,2,1,0:T(8,128)(2,1)} %bitcast.7, bf16[48,2,2,128,256]{4,3,2,1,0:T(8,128)(2,1)} %bitcast.6), custom_call_target="tpu_custom_call" | custom-call | bytes 31850496 | tf_op jit(solution)/shard_map/pack_parcels/pallas_call | solution.py:88
  13.7 0.0 collective-permute-done.1
  13.7 0.0 collective-permute-done
  13.7 252.7 %all_to_all.5.got_ref = bf16[128,648,128]{2,1,0:T(8,128)(2,1)} all-to-all(bf16[128,648,128]{2,1,0:T(8,128)(2,1)} %pack_parcels.1), channel_id=1, replica_groups=mesh['sec'=64,'mpo'=2] {'sec','mpo'}, dimensions={0} | all-to-all | bytes 42467328 | tf_op jit(solution)/shard_map/all_to_all | solution.py:322
  266.5 3.6 %theta_quarters.1 = (bf16[128,64,128]{2,1,0:T(8,128)(2,1)}, bf16[128,64,128]{2,1,0:T(8,128)(2,1)S(1)}) custom-call(bf16[128,648,128]{2,1,0:T(8,128)(2,1)} %all_to_all.5.got_ref), custom_call_target="tpu_custom_call" | custom-call | bytes 8388608 | tf_op jit(solution)/shard_map/theta_quarters/pallas_call | solution.py:132
  270.1 0.5 collective-permute-start.2
  270.5 0.0 copy-start.1
  270.5 0.0 copy-start
  270.5 0.1 collective-permute-start.3
  270.7 2.0 places.1.places_ref
  272.7 0.0 copy-done.1
  272.7 0.6 add_bitcast_fusion.pairs_ref
  273.3 0.0 copy-done
  273.4 0.9 pad_maximum_fusion
  274.3 2.2 collective-permute-done.2.refs_0_
  276.5 1.0 collective-permute-done.3.refs_1_
  277.5 15.7 %contract.1 = bf16[128,48,256]{2,1,0:T(8,128)(2,1)} custom-call(s32[2,128]{1,0:T(2,128)} %places.1.places_ref, s32[4,48]{1,0:T(4,128)} %add_bitcast_fusion.pairs_ref, s32[1]{0:T(128)} %bitcast.core_ref, bf16[128,648,128]{2,1,0:T(8,128)(2,1)} %all_to_all.5.got_ref, bf16[128,64,128]{2,1,0:T(8,128)(2,1)} %collective-permute-done.2.refs_0_, ...), custom_call_target="tpu_custom_call" | custom-call | flops 6442450944 | bytes 22020096 | tf_op jit(solution)/shard_map/contract/pallas_call | solution.py:283
  (2 shorter events, 0.0 us)
Async XLA Ops:
  0.0 13.7 %collective-permute-start = (bf16[2,256,256]{2,1,0:T(8,128)(2,1)}, bf16[2,256,256]{2,1,0:T(8,128)(2,1)S(1)}, u32[]{:S(2)}, u32[]{:S(2)}) collective-permute-start(bf16[2,256,256]{2,1,0:T(8,128)(2,1)} %param.13), channel_id=1, source_target_pairs={{0,1},{1,0},{2,3},{3,2},{4,5},{5,4},{6,7},{7,6},{8,9},{9,8},{10,11... | collective-permute-start | bytes 786440 | tf_op jit(solution)/shard_map/ppermute | solution.py:314
  0.7 13.1 %collective-permute-start.1 = (s32[48,2]{0,1:T(2,128)}, s32[48,2]{0,1:T(2,128)S(1)}, u32[]{:S(2)}, u32[]{:S(2)}) collective-permute-start(s32[48,2]{0,1:T(2,128)} %param.10), channel_id=1, source_target_pairs={{0,1},{1,0},{2,3},{3,2},{4,5},{5,4},{6,7},{7,6},{8,9},{9,8},{10,11... | collective-permute-start | bytes 1160 | tf_op jit(solution)/shard_map/ppermute | solution.py:315
  270.1 6.4 %collective-permute-start.2 = (bf16[128,64,128]{2,1,0:T(8,128)(2,1)}, bf16[128,64,128]{2,1,0:T(8,128)(2,1)}, u32[]{:S(2)}, u32[]{:S(2)}) collective-permute-start(bf16[128,64,128]{2,1,0:T(8,128)(2,1)} %get-tuple-element.20), channel_id=1, source_target_pairs={{0,1},{1,0},{2,3},{3,2},{4,5},{5,4},{6,7},{7,6},{8,9},{9,8},{10,11... | collective-permute-start | bytes 6291464 | tf_op jit(solution)/shard_map/ppermute | solution.py:329
  270.5 2.2 copy-start.1
  270.5 2.8 copy-start
  270.5 6.9 %collective-permute-start.3 = (bf16[128,64,128]{2,1,0:T(8,128)(2,1)S(1)}, bf16[128,64,128]{2,1,0:T(8,128)(2,1)}, u32[]{:S(2)}, u32[]{:S(2)}) collective-permute-start(bf16[128,64,128]{2,1,0:T(8,128)(2,1)S(1)} %get-tuple-element.21), channel_id=1, source_target_pairs={{0,1},{1,0},{2,3},{3,2},{4,5},{5,4},{6,7},{7,6},{8,9},{9,8},{10,11... | collective-permute-start | bytes 6291464 | tf_op jit(solution)/shard_map/ppermute | solution.py:329

commit v7 on v6

--- a/solution.py
+++ b/solution.py
@@ -176,8 +176,9 @@
 
 
 def apply_kernel(sides, places_ref, pairs_ref, core_ref, got_ref, *refs):
-    others_ref, right_ref, out_ref = refs[:sides], refs[sides], refs[sides + 1]
-    theta, left, inner, even, odd, turned, theta_sems, left_sems, out_sems = refs[sides + 2:]
+    others_ref, right_hbm, out_ref = refs[:sides], refs[sides], refs[sides + 1]
+    theta, left, inner, even, odd, turned, right_ref = refs[sides + 2:sides + 9]
+    theta_sems, left_sems, out_sems, right_sem = refs[sides + 9:]
     slots, _, _, quarter, cols = theta.shape
     half, tile, bulk = 2 * quarter, 4 * quarter, left.shape[2]
     channels = 2 * bulk // half
@@ -200,6 +201,8 @@
         return carry
 
     lax.fori_loop(0, slots, fetch, 0)
+    fetch_right = copy(right_hbm, right_ref, right_sem)
+    fetch_right.start()
 
     strip = 16
     strip_rows = lax.broadcasted_iota(jnp.int32, (strip, cols), 0)
@@ -226,6 +229,7 @@
         return lax.fori_loop(live // strip, tile // strip, clear, carry)
 
     lax.fori_loop(0, slots, trim, 0)
+    fetch_right.wait()
 
     half_ids = lax.broadcasted_iota(jnp.int32, (half, cols), 0) + core * half
 
@@ -285,7 +289,7 @@
         grid_spec=pltpu.PrefetchScalarGridSpec(
             num_scalar_prefetch=3,
             grid=(),
-            in_specs=[HBM] * (1 + len(others)) + [pl.BlockSpec(memory_space=pltpu.VMEM)],
+            in_specs=[HBM] * (2 + len(others)),
             out_specs=HBM,
             scratch_shapes=[
                 pltpu.VMEM((slots, 2, 2, quarter, cols), dtype),
@@ -294,9 +298,11 @@
                 pltpu.VMEM((GROUP, half, cols), jnp.float32),
                 pltpu.VMEM((GROUP, half, cols), jnp.float32),
                 pltpu.VMEM((slots // GROUP, half, GROUP, cols), dtype),
+                pltpu.VMEM((channels * tile, cols), dtype),
                 pltpu.SemaphoreType.DMA((slots,)),
                 pltpu.SemaphoreType.DMA((slots,)),
                 pltpu.SemaphoreType.DMA((slots // GROUP,)),
+                pltpu.SemaphoreType.DMA,
             ],
         ),
         out_shape=jax.ShapeDtypeStruct((half, slots, cols), dtype),

time: 293 us -> 293 us (level)
  no operation moved by 1% of the time
where the time goes in v7:
time: 293 us; the launch traced here: 292 us
  blocking collectives  253 us (86%)
  Pallas kernels  33.5 us (11%)
  waiting for transfers between devices  3.19 us (1%)
    all_to_all x1, blocking collectives, on_device(): lax.all_to_all(parcels, ('sec', 'mpo'), split_axis=0, concat_axis=0, tile...  253 us
    pallas_call x1, Pallas kernels, apply(): pl.pallas_call(functools.partial(apply_kernel, cols // LANES), grid_spec=...  14.9 us
    pallas_call x1, Pallas kernels, pack(): pl.pallas_call(pack_kernel, grid_spec=pltpu.PrefetchScalarGridSpec(num_sc...  13 us
  transfers between devices with their start and end apart: 4, of which 2 were waited for; matrix products, arithmetic and copies ran while one was open for 1% of the time, Pallas kernels for 5%

profile of v7, /device:TPU:11, one launch (start us, length us, event | category | flops | bytes accessed | tf_op | source)
XLA Modules:
  0.0 292.3 jit_solution(10668583432904527518)
XLA Ops:
  0.0 0.7 collective-permute-start
  0.7 0.0 collective-permute-start.1
  0.7 13.0 %pack_parcels.1 = bf16[128,648,128]{2,1,0:T(8,128)(2,1)} custom-call(s32[48]{0:T(128)} %owner_ref.1, s32[48]{0:T(128)} %slot_ref.1, s32[48]{0:T(128)} %dims_ref.1, s32[1]{0:T(128)} %bitcast.core_ref, bf16[48,2,2,64,256]{4,3,2,1,0:T(8,128)(2,1)} %bitcast.7, bf16[48,2,2,128,256]{4,3,2,1,0:T(8,128)(2,1)} %bitcast.6), custom_call_target="tpu_custom_call" | custom-call | bytes 31850496 | tf_op jit(solution)/shard_map/pack_parcels/pallas_call | solution.py:88
  13.7 0.0 collective-permute-done.1
  13.7 0.0 collective-permute-done
  13.7 252.8 %all_to_all.5.got_ref = bf16[128,648,128]{2,1,0:T(8,128)(2,1)} all-to-all(bf16[128,648,128]{2,1,0:T(8,128)(2,1)} %pack_parcels.1), channel_id=1, replica_groups=mesh['sec'=64,'mpo'=2] {'sec','mpo'}, dimensions={0} | all-to-all | bytes 42467328 | tf_op jit(solution)/shard_map/all_to_all | solution.py:328
  266.5 3.6 %theta_quarters.1 = (bf16[128,64,128]{2,1,0:T(8,128)(2,1)}, bf16[128,64,128]{2,1,0:T(8,128)(2,1)S(1)}) custom-call(bf16[128,648,128]{2,1,0:T(8,128)(2,1)} %all_to_all.5.got_ref), custom_call_target="tpu_custom_call" | custom-call | bytes 8388608 | tf_op jit(solution)/shard_map/theta_quarters/pallas_call | solution.py:132
  270.1 0.5 collective-permute-start.2
  270.5 0.0 copy-start.1
  270.5 0.0 copy-start
  270.5 0.1 collective-permute-start.3
  270.7 2.0 places.1.places_ref
  272.7 0.0 copy-done.1
  272.7 0.6 add_bitcast_fusion.pairs_ref
  273.3 0.0 copy-done
  273.3 0.9 pad_maximum_fusion
  274.3 2.2 collective-permute-done.2.refs_0_
  276.5 1.0 collective-permute-done.3.refs_1_
  277.4 14.9 %contract.1 = bf16[128,48,256]{2,1,0:T(8,128)(2,1)} custom-call(s32[2,128]{1,0:T(2,128)} %places.1.places_ref, s32[4,48]{1,0:T(4,128)} %add_bitcast_fusion.pairs_ref, s32[1]{0:T(128)} %bitcast.core_ref, bf16[128,648,128]{2,1,0:T(8,128)(2,1)} %all_to_all.5.got_ref, bf16[128,64,128]{2,1,0:T(8,128)(2,1)} %collective-permute-done.2.refs_0_, ...), custom_call_target="tpu_custom_call" | custom-call | flops 6442450944 | bytes 22020096 | tf_op jit(solution)/shard_map/contract/pallas_call | solution.py:287
  (2 shorter events, 0.0 us)
Async XLA Ops:
  0.0 13.7 %collective-permute-start = (bf16[2,256,256]{2,1,0:T(8,128)(2,1)}, bf16[2,256,256]{2,1,0:T(8,128)(2,1)S(1)}, u32[]{:S(2)}, u32[]{:S(2)}) collective-permute-start(bf16[2,256,256]{2,1,0:T(8,128)(2,1)} %param.13), channel_id=1, source_target_pairs={{0,1},{1,0},{2,3},{3,2},{4,5},{5,4},{6,7},{7,6},{8,9},{9,8},{10,11... | collective-permute-start | bytes 786440 | tf_op jit(solution)/shard_map/ppermute | solution.py:320
  0.7 13.0 %collective-permute-start.1 = (s32[48,2]{0,1:T(2,128)}, s32[48,2]{0,1:T(2,128)S(1)}, u32[]{:S(2)}, u32[]{:S(2)}) collective-permute-start(s32[48,2]{0,1:T(2,128)} %param.10), channel_id=1, source_target_pairs={{0,1},{1,0},{2,3},{3,2},{4,5},{5,4},{6,7},{7,6},{8,9},{9,8},{10,11... | collective-permute-start | bytes 1160 | tf_op jit(solution)/shard_map/ppermute | solution.py:321
  270.1 6.4 %collective-permute-start.2 = (bf16[128,64,128]{2,1,0:T(8,128)(2,1)}, bf16[128,64,128]{2,1,0:T(8,128)(2,1)}, u32[]{:S(2)}, u32[]{:S(2)}) collective-permute-start(bf16[128,64,128]{2,1,0:T(8,128)(2,1)} %get-tuple-element.20), channel_id=1, source_target_pairs={{0,1},{1,0},{2,3},{3,2},{4,5},{5,4},{6,7},{7,6},{8,9},{9,8},{10,11... | collective-permute-start | bytes 6291464 | tf_op jit(solution)/shard_map/ppermute | solution.py:335
  270.5 2.2 copy-start.1
  270.5 2.8 copy-start
  270.5 6.9 %collective-permute-start.3 = (bf16[128,64,128]{2,1,0:T(8,128)(2,1)S(1)}, bf16[128,64,128]{2,1,0:T(8,128)(2,1)}, u32[]{:S(2)}, u32[]{:S(2)}) collective-permute-start(bf16[128,64,128]{2,1,0:T(8,128)(2,1)S(1)} %get-tuple-element.21), channel_id=1, source_target_pairs={{0,1},{1,0},{2,3},{3,2},{4,5},{5,4},{6,7},{7,6},{8,9},{9,8},{10,11... | collective-permute-start | bytes 6291464 | tf_op jit(solution)/shard_map/ppermute | solution.py:335

commit v8 on v7

--- a/solution.py
+++ b/solution.py
@@ -114,16 +114,32 @@
 
 
 def split_kernel(first, got_ref, *refs):
-    outs_ref, sems = refs[:-1], refs[-1]
+    outs_ref, (staged, read_sems, write_sems) = refs[:-3], refs[-3:]
     quarter = outs_ref[0].shape[1]
-    moves = [
-        copy(got_ref.at[:, pl.ds(first + c * quarter, quarter)], out_ref, sems.at[c])
+    parts = read_sems.shape[0]
+    size = staged.shape[0] // parts
+    spans = [pl.ds(p * size, size) for p in range(parts)]
+    reads = [
+        copy(got_ref.at[span, pl.ds(first, staged.shape[1])], staged.at[span], read_sems.at[p])
+        for p, span in enumerate(spans)
+    ]
+    writes = [
+        copy(
+            staged.at[span, pl.ds(c * quarter, quarter)],
+            out_ref.at[span],
+            write_sems.at[p, c],
+        )
+        for p, span in enumerate(spans)
         for c, out_ref in enumerate(outs_ref)
     ]
-    for move in moves:
-        move.start()
-    for move in moves:
-        move.wait()
+    for read in reads:
+        read.start()
+    for p in range(parts):
+        reads[p].wait()
+        for c in range(len(outs_ref)):
+            writes[p * len(outs_ref) + c].start()
+    for write in writes:
+        write.wait()
 
 
 def split(got, first, quarter, sides):
@@ -132,10 +148,14 @@
     return pl.pallas_call(
         functools.partial(split_kernel, first),
         in_specs=[HBM],
-        out_specs=[pl.BlockSpec(memory_space=pltpu.VMEM)] * sides,
-        scratch_shapes=[pltpu.SemaphoreType.DMA((sides,))],
+        out_specs=[HBM] * sides,
+        scratch_shapes=[
+            pltpu.VMEM((parcels, sides * quarter, LANES), got.dtype),
+            pltpu.SemaphoreType.DMA((8,)),
+            pltpu.SemaphoreType.DMA((8, sides)),
+        ],
         out_shape=[part] * sides,
-        compiler_params=pltpu.CompilerParams(vmem_limit_bytes=44 << 20),
+        compiler_params=pltpu.CompilerParams(vmem_limit_bytes=60 << 20),
         cost_estimate=pl.CostEstimate(flops=0, bytes_accessed=8 << 20, transcendentals=0),
         name="theta_quarters",
     )(got)
@@ -271,11 +291,21 @@
         if g > 0:
             write(g - 1).start()
 
+    def write_part(b):
+        rows = pl.ds(b * part, part)
+        return copy(
+            turned.at[groups - 1, rows],
+            out_ref.at[rows, pl.ds((groups - 1) * GROUP, GROUP)],
+            out_sems.at[groups - 1 + b],
+        )
+
     for b in range(steps):
         turn(groups - 1, b)
-    write(groups - 1).start()
-    for g in range(groups):
+        write_part(b).start()
+    for g in range(groups - 1):
         write(g).wait()
+    for b in range(steps):
+        write_part(b).wait()
 
 
 def apply(places, pairs, core, got, others, right, dtype):
@@ -301,7 +331,7 @@
                 pltpu.VMEM((channels * tile, cols), dtype),
                 pltpu.SemaphoreType.DMA((slots,)),
                 pltpu.SemaphoreType.DMA((slots,)),
-                pltpu.SemaphoreType.DMA((slots // GROUP,)),
+                pltpu.SemaphoreType.DMA((slots // GROUP + GROUP // STEP - 1,)),
                 pltpu.SemaphoreType.DMA,
             ],
         ),

time: 293 us -> 293 us (level)
  no operation moved by 1% of the time
where the time goes in v8:
time: 293 us; the launch traced here: 292 us
  blocking collectives  253 us (86%)
  Pallas kernels  33.4 us (11%)
  waiting for transfers between devices  3.48 us (1%)
    all_to_all x1, blocking collectives, on_device(): lax.all_to_all(parcels, ('sec', 'mpo'), split_axis=0, concat_axis=0, tile...  253 us
    pallas_call x1, Pallas kernels, apply(): pl.pallas_call(functools.partial(apply_kernel, cols // LANES), grid_spec=...  14.6 us
    pallas_call x1, Pallas kernels, pack(): pl.pallas_call(pack_kernel, grid_spec=pltpu.PrefetchScalarGridSpec(num_sc...  13 us
  transfers between devices with their start and end apart: 4, of which 2 were waited for; matrix products, arithmetic and copies ran while one was open for 1% of the time, Pallas kernels for 5%

profile of v8, /device:TPU:11, one launch (start us, length us, event | category | flops | bytes accessed | tf_op | source)
XLA Modules:
  0.0 292.4 jit_solution(271888545218208645)
XLA Ops:
  0.0 0.7 collective-permute-start
  0.7 0.0 collective-permute-start.1
  0.7 13.0 %pack_parcels.1 = bf16[128,648,128]{2,1,0:T(8,128)(2,1)} custom-call(s32[48]{0:T(128)} %owner_ref.1, s32[48]{0:T(128)} %slot_ref.1, s32[48]{0:T(128)} %dims_ref.1, s32[1]{0:T(128)} %bitcast.core_ref, bf16[48,2,2,64,256]{4,3,2,1,0:T(8,128)(2,1)} %bitcast.7, bf16[48,2,2,128,256]{4,3,2,1,0:T(8,128)(2,1)} %bitcast.6), custom_call_target="tpu_custom_call" | custom-call | bytes 31850496 | tf_op jit(solution)/shard_map/pack_parcels/pallas_call | solution.py:88
  13.7 0.0 collective-permute-done.1
  13.7 0.0 collective-permute-done
  13.7 252.7 %all_to_all.5.got_ref = bf16[128,648,128]{2,1,0:T(8,128)(2,1)} all-to-all(bf16[128,648,128]{2,1,0:T(8,128)(2,1)} %pack_parcels.1), channel_id=1, replica_groups=mesh['sec'=64,'mpo'=2] {'sec','mpo'}, dimensions={0} | all-to-all | bytes 42467328 | tf_op jit(solution)/shard_map/all_to_all | solution.py:358
  266.5 3.7 %theta_quarters.1 = (bf16[128,64,128]{2,1,0:T(8,128)(2,1)}, bf16[128,64,128]{2,1,0:T(8,128)(2,1)}) custom-call(bf16[128,648,128]{2,1,0:T(8,128)(2,1)} %all_to_all.5.got_ref), custom_call_target="tpu_custom_call" | custom-call | bytes 8388608 | tf_op jit(solution)/shard_map/theta_quarters/pallas_call | solution.py:148
  270.2 0.5 collective-permute-start.2
  270.6 0.0 copy-start.2
  270.7 0.0 copy-start.1
  270.7 0.1 collective-permute-start.3
  270.8 2.0 places.1.places_ref
  272.8 0.0 copy-done.2
  272.8 0.6 add_bitcast_fusion.pairs_ref
  273.4 0.0 copy-done.1
  273.5 0.9 pad_maximum_fusion
  274.3 2.1 collective-permute-done.2.refs_0_
  276.4 0.0 copy-start
  276.4 1.3 collective-permute-done.3.refs_1_
  277.8 0.0 copy-done
  277.8 14.6 %contract.1 = bf16[128,48,256]{2,1,0:T(8,128)(2,1)} custom-call(s32[2,128]{1,0:T(2,128)} %places.1.places_ref, s32[4,48]{1,0:T(4,128)} %add_bitcast_fusion.pairs_ref, s32[1]{0:T(128)} %bitcast.core_ref, bf16[128,648,128]{2,1,0:T(8,128)(2,1)} %all_to_all.5.got_ref, bf16[128,64,128]{2,1,0:T(8,128)(2,1)} %copy-done, ...), custom_call_target="tpu_custom_call" | custom-call | flops 6442450944 | bytes 22020096 | tf_op jit(solution)/shard_map/contract/pallas_call | solution.py:317
  (2 shorter events, 0.0 us)
Async XLA Ops:
  0.0 13.7 %collective-permute-start = (bf16[2,256,256]{2,1,0:T(8,128)(2,1)}, bf16[2,256,256]{2,1,0:T(8,128)(2,1)S(1)}, u32[]{:S(2)}, u32[]{:S(2)}) collective-permute-start(bf16[2,256,256]{2,1,0:T(8,128)(2,1)} %param.13), channel_id=1, source_target_pairs={{0,1},{1,0},{2,3},{3,2},{4,5},{5,4},{6,7},{7,6},{8,9},{9,8},{10,11... | collective-permute-start | bytes 786440 | tf_op jit(solution)/shard_map/ppermute | solution.py:350
  0.7 13.1 %collective-permute-start.1 = (s32[48,2]{0,1:T(2,128)}, s32[48,2]{0,1:T(2,128)S(1)}, u32[]{:S(2)}, u32[]{:S(2)}) collective-permute-start(s32[48,2]{0,1:T(2,128)} %param.10), channel_id=1, source_target_pairs={{0,1},{1,0},{2,3},{3,2},{4,5},{5,4},{6,7},{7,6},{8,9},{9,8},{10,11... | collective-permute-start | bytes 1160 | tf_op jit(solution)/shard_map/ppermute | solution.py:351
  270.2 6.3 %collective-permute-start.2 = (bf16[128,64,128]{2,1,0:T(8,128)(2,1)}, bf16[128,64,128]{2,1,0:T(8,128)(2,1)S(1)}, u32[]{:S(2)}, u32[]{:S(2)}) collective-permute-start(bf16[128,64,128]{2,1,0:T(8,128)(2,1)} %get-tuple-element.20), channel_id=1, source_target_pairs={{0,1},{1,0},{2,3},{3,2},{4,5},{5,4},{6,7},{7,6},{8,9},{9,8},{10,11... | collective-permute-start | bytes 6291464 | tf_op jit(solution)/shard_map/ppermute | solution.py:365
  270.6 2.1 copy-start.2
  270.7 2.8 copy-start.1
  270.7 7.1 %collective-permute-start.3 = (bf16[128,64,128]{2,1,0:T(8,128)(2,1)}, bf16[128,64,128]{2,1,0:T(8,128)(2,1)}, u32[]{:S(2)}, u32[]{:S(2)}) collective-permute-start(bf16[128,64,128]{2,1,0:T(8,128)(2,1)} %get-tuple-element.21), channel_id=1, source_target_pairs={{0,1},{1,0},{2,3},{3,2},{4,5},{5,4},{6,7},{7,6},{8,9},{9,8},{10,11... | collective-permute-start | bytes 6291464 | tf_op jit(solution)/shard_map/ppermute | solution.py:365
  276.4 1.3 copy-start
